TPU v7x, 128 devices: a whole 4x4x4 slice. The times are simulated.
128 devices in a mesh: dp: 64 (over z, x, y_lo, core), mp: 2 (over y_hi).
Axes of the slice: x: 4, y: 4 (y_hi: 2, y_lo: 2; y = y_hi * 2 + y_lo), z: 4, core: 2. Of those that a mesh axis runs over, the one named last changes fastest.
Arguments:
- code_tokens: int32 [32768], P('dp'), may hold values from 0 to 2047
- segments: int32 [32768], P('dp'), may hold values from 0 to 4, as said below
- layout: int32 [8, 8], replicated, may hold values from 0 to 1, as said below
- durations: int32 [256], P('dp'), may hold values from 2048 to 49149
- overflow: int32 [64], P('dp'), may hold values from 0 to 1, as said below
- upper_context: bfloat16 [32768, 1024], P('dp', 'mp'), may hold values from -6 to 6
- embed_table: bfloat16 [2048, 1024], P(None, 'mp'), may hold values from -6 to 6
- condition_weight: bfloat16 [1024, 1024], P(None, 'mp'), may hold values from -0.1875 to 0.1875
- attention_weight: bfloat16 [4, 1024, 1024], P(None, None, 'mp')
- feedforward_weight: bfloat16 [2, 1024, 4096], P(None, None, 'mp'), may hold values from -0.1875 to 0.1875
- output_table: bfloat16 [1024, 2048], P(None, 'mp')
- norm_gains: float32 [6, 1024], replicated
- embed_master: float32 [2048, 1024], P('dp', 'mp'), may hold values from -6 to 6
- condition_master: float32 [1024, 1024], P('dp', 'mp'), may hold values from -0.1875 to 0.1875
- attention_master: float32 [4, 1024, 1024], P(None, 'dp', 'mp'), may hold values from -0.1875 to 0.1875
- feedforward_master: float32 [2, 1024, 4096], P(None, 'dp', 'mp'), may hold values from -0.1875 to 0.1875
- output_master: float32 [1024, 2048], P('dp', 'mp'), may hold values from -0.1875 to 0.1875
- norms_master: float32 [6, 1024], P(None, 'dp')
- embed_first: float32 [2048, 1024], P('dp', 'mp'), may hold values from -2.2888184e-05 to 2.2888184e-05
- condition_first: float32 [1024, 1024], P('dp', 'mp'), may hold values from -0.00036621094 to 0.00036621094
- attention_first: float32 [4, 1024, 1024], P(None, 'dp', 'mp'), may hold values from -0.00036621094 to 0.00036621094
- feedforward_first: float32 [2, 1024, 4096], P(None, 'dp', 'mp'), may hold values from -0.00036621094 to 0.00036621094
- output_first: float32 [1024, 2048], P('dp', 'mp'), may hold values from -0.00036621094 to 0.00036621094
- norms_first: float32 [6, 1024], P(None, 'dp'), may hold values from -0.0014648438 to 0.0014648438
- embed_second: float32 [2048, 1024], P('dp', 'mp'), may hold values from 4.598491e-11 to 1.8506123e-10
- condition_second: float32 [1024, 1024], P('dp', 'mp'), may hold values from 2.9497638e-09 to 1.1804663e-08
- attention_second: float32 [4, 1024, 1024], P(None, 'dp', 'mp'), may hold values from 2.9497638e-09 to 1.1804663e-08
- feedforward_second: float32 [2, 1024, 4096], P(None, 'dp', 'mp'), may hold values from 2.9497638e-09 to 1.1804663e-08
- output_second: float32 [1024, 2048], P('dp', 'mp'), may hold values from 2.9497638e-09 to 1.1804663e-08
- norms_second: float32 [6, 1024], P(None, 'dp'), may hold values from 4.7106496e-08 to 1.8898677e-07
Outputs:
- loss_sum: float32 [], replicated
- clip_seconds: float32 [], replicated
- gradient_norm: float32 [], replicated
- embed_moment: float32 [2048, 1024], P('dp', 'mp')
- embed_variance: float32 [2048, 1024], P('dp', 'mp')
- embed_updated: float32 [2048, 1024], P('dp', 'mp')
- condition_moment: float32 [1024, 1024], P('dp', 'mp')
- condition_variance: float32 [1024, 1024], P('dp', 'mp')
- condition_updated: float32 [1024, 1024], P('dp', 'mp')
- attention_moment: float32 [4, 1024, 1024], P(None, 'dp', 'mp')
- attention_variance: float32 [4, 1024, 1024], P(None, 'dp', 'mp')
- attention_updated: float32 [4, 1024, 1024], P(None, 'dp', 'mp')
- feedforward_moment: float32 [2, 1024, 4096], P(None, 'dp', 'mp')
- feedforward_variance: float32 [2, 1024, 4096], P(None, 'dp', 'mp')
- feedforward_updated: float32 [2, 1024, 4096], P(None, 'dp', 'mp')
- output_moment: float32 [1024, 2048], P('dp', 'mp')
- output_variance: float32 [1024, 2048], P('dp', 'mp')
- output_updated: float32 [1024, 2048], P('dp', 'mp')
- norms_moment: float32 [6, 1024], P(None, 'dp')
- norms_variance: float32 [6, 1024], P(None, 'dp')
- norms_updated: float32 [6, 1024], P(None, 'dp')
Inputs may be any that keep to these rules, and one draw needn't show every extreme that they name: `segments`: within each window the clip numbers never fall, run through 0 to 3 with every clip present, and may be followed by padding marked 4; at least 8 tokens of each window are no padding. `layout`: the diagonal is 1 and entries above it are 0. `overflow`: at least one window is kept (flag 0).
All inputs are finite; a program needn't handle non-finite values.
Results may differ from a plain program's by a relative error of at most 0.015.
Values sent between devices are 32-bit elements; how exact they have to be, the bound alone decides.
No kernel may reach another device: no remote copies, remote signals or barrier semaphores. Data moves between devices by JAX's collectives and lax.ppermute only.
A program may use at most 192 MiB of HBM per device.

v0:
```python
import jax
import jax.numpy as jnp
from jax import lax
from jax.sharding import PartitionSpec as P

HEAD_DIM = 64
BLK = 64
CLIPS_DEV = 4
STEP = 10


LAYER_EPS = 1e-05
SAMPLE_RATE = 44100.0
LOG_TWO_NATS = 0.6931471805599453
CLIP_NORM = 1.0
BETA_FIRST = 0.9
BETA_SECOND = 0.95
ADAM_EPSILON = 1e-08
WEIGHT_DECAY = 0.01
RATE_MATRIX = 0.1
RATE_TABLE = 1.0
RATE_NORMS = 1.0


def merged_2(value, axis, join):
    pieces = jax.tree.map(lambda part: lax.all_gather(part, axis), value)
    head = jax.tree.map(lambda part: part[0], pieces)
    tail = jax.tree.map(lambda part: part[1:], pieces)
    running, _ = lax.scan(lambda running, piece: (join(running, piece), None), head, tail)
    return running


def contract(left_side, right_side, left_dim, right_dim):
    return lax.dot_general(
        left_side,
        right_side,
        (((left_dim,), (right_dim,)), ((), ())),
        preferred_element_type=jnp.float32,
    )


def norm_rows(values, gain_row, shift_row):
    average = jnp.mean(values, axis=-1, keepdims=True)
    centred = values - average
    variance = jnp.mean(centred * centred, axis=-1, keepdims=True)
    return centred * lax.rsqrt(variance + LAYER_EPS) * gain_row + shift_row


def allowed_mask(segments, layout):
    length = segments.shape[0]
    position = jnp.arange(length)
    blocks = layout.shape[0]
    block_open = (
        jnp.broadcast_to(layout[:, None, :, None], (blocks, BLK, blocks, BLK)).reshape(
            length, length
        )
        > 0
    )
    causal = position[None, :] <= position[:, None]
    return causal & (segments[:, None] == segments[None, :]) & block_open


def masked_scores(queries, keys_low, allowed):
    scores = jnp.einsum(
        "qhd,khd->hqk", queries, keys_low, preferred_element_type=jnp.float32
    ) * HEAD_DIM ** (-0.5)
    return jnp.where(allowed[None], scores, -1e30)


def merge_stats(first_part, second_part):
    row_top = jnp.maximum(first_part[0], second_part[0])
    row_sums = first_part[1] * jnp.exp(first_part[0] - row_top) + second_part[1] * jnp.exp(
        second_part[0] - row_top
    )
    return (row_top, row_sums, first_part[2] + second_part[2])


def layer_forward(residual, attention_weight, feedforward_weight, norm_gains, allowed):
    length = residual.shape[0]
    heads_local = attention_weight.shape[2] // HEAD_DIM
    normed_one = norm_rows(residual, norm_gains[0], norm_gains[1]).astype(jnp.bfloat16)
    projected = jnp.einsum(
        "td,sde->ste", normed_one, attention_weight[:3], preferred_element_type=jnp.float32
    ).astype(jnp.bfloat16)
    heads_view = projected.reshape(3, length, heads_local, HEAD_DIM)
    masked = masked_scores(heads_view[0], heads_view[1], allowed)
    row_top = jnp.max(masked, axis=-1, keepdims=True)
    exponents = jnp.exp(masked - row_top)
    row_sums = jnp.sum(exponents, axis=-1, keepdims=True)
    attend_low = (exponents / row_sums).astype(jnp.bfloat16)
    log_total = row_top + jnp.log(row_sums)
    mixed_low = (
        jnp.einsum("hqk,khd->qhd", attend_low, heads_view[2], preferred_element_type=jnp.float32)
        .astype(jnp.bfloat16)
        .reshape(length, -1)
    )
    after_attention = residual + lax.psum(contract(mixed_low, attention_weight[3], 1, 1), "mp")
    normed_two = norm_rows(after_attention, norm_gains[2], norm_gains[3]).astype(jnp.bfloat16)
    pre_act = jnp.dot(normed_two, feedforward_weight[0], preferred_element_type=jnp.float32)
    activated = jax.nn.gelu(pre_act).astype(jnp.bfloat16)
    after_block = after_attention + lax.psum(contract(activated, feedforward_weight[1], 1, 1), "mp")
    saved_state = (
        residual,
        normed_one,
        heads_view,
        log_total,
        mixed_low,
        after_attention,
        normed_two,
        pre_act,
        activated,
    )
    return (after_block, saved_state)


def head_loss(after_block, output_table, norm_gains, code_tokens, segments, keep_flag, model_rank):
    normed_three = norm_rows(after_block, norm_gains[4], norm_gains[5]).astype(jnp.bfloat16)
    logits = jnp.dot(normed_three, output_table, preferred_element_type=jnp.float32)
    half_vocab = output_table.shape[1]
    targets = jnp.concatenate([code_tokens[1:], code_tokens[-1:]])
    target_hit = jnp.arange(half_vocab)[None, :] == (targets - model_rank * half_vocab)[:, None]
    row_top = jnp.max(logits, axis=1)
    row_sums = jnp.sum(jnp.exp(logits - row_top[:, None]), axis=1)
    picked = jnp.sum(jnp.where(target_hit, logits, 0.0), axis=1)
    merged = merged_2((row_top, row_sums, picked), "mp", merge_stats)
    log_norm = merged[0] + jnp.log(merged[1])
    next_segment = jnp.concatenate([segments[1:], jnp.full((1,), -1, jnp.int32)])
    counted = ((segments == next_segment) & (segments < CLIPS_DEV)).astype(jnp.float32) * keep_flag
    loss_local = jnp.sum(counted * (log_norm - merged[2])) / LOG_TWO_NATS
    grad_logits = (counted / LOG_TWO_NATS)[:, None] * (
        jnp.exp(logits - log_norm[:, None]) - target_hit.astype(jnp.float32)
    )
    grad_low = grad_logits.astype(jnp.bfloat16)
    output_grad = contract(normed_three, grad_low, 0, 0)
    grad_normed = lax.psum(contract(grad_low, output_table, 1, 1), "mp")
    _, pullback = jax.vjp(norm_rows, after_block, norm_gains[4], norm_gains[5])
    grad_input, grad_gain, grad_shift = pullback(grad_normed)
    return (loss_local, grad_input, output_grad, (grad_gain, grad_shift))


def feedforward_backward(grad_block, saved_state, feedforward_weight, norm_gains):
    after_attention, normed_two, pre_act, activated = saved_state[5:]
    branch_low = grad_block.astype(jnp.bfloat16)
    down_grad = contract(branch_low, activated, 0, 0)
    grad_activated = jnp.dot(branch_low, feedforward_weight[1], preferred_element_type=jnp.float32)
    _, gelu_pull = jax.vjp(jax.nn.gelu, pre_act)
    grad_pre = gelu_pull(grad_activated)[0].astype(jnp.bfloat16)
    up_grad = contract(normed_two, grad_pre, 0, 0)
    grad_normed = lax.psum(contract(grad_pre, feedforward_weight[0], 1, 1), "mp")
    _, pullback = jax.vjp(norm_rows, after_attention, norm_gains[2], norm_gains[3])
    grad_input, grad_gain, grad_shift = pullback(grad_normed)
    return (grad_block + grad_input, jnp.stack([up_grad, down_grad]), (grad_gain, grad_shift))


def attention_backward(grad_attention, saved_state, attention_weight, norm_gains, allowed):
    residual, normed_one, heads_view, log_total, mixed_low = saved_state[:5]
    length = residual.shape[0]
    heads_local = heads_view.shape[2]
    branch_low = grad_attention.astype(jnp.bfloat16)
    output_grad = contract(branch_low, mixed_low, 0, 0)
    grad_mixed = (
        jnp.dot(branch_low, attention_weight[3], preferred_element_type=jnp.float32)
        .astype(jnp.bfloat16)
        .reshape(length, heads_local, HEAD_DIM)
    )
    masked = masked_scores(heads_view[0], heads_view[1], allowed)
    attend_full = jnp.exp(masked - log_total)
    attend_low = attend_full.astype(jnp.bfloat16)
    grad_values = jnp.einsum(
        "hqk,qhd->khd", attend_low, grad_mixed, preferred_element_type=jnp.float32
    )
    grad_attend = jnp.einsum(
        "qhd,khd->hqk", grad_mixed, heads_view[2], preferred_element_type=jnp.float32
    )
    grad_scores = (
        attend_full * (grad_attend - jnp.sum(attend_full * grad_attend, axis=-1, keepdims=True))
    ).astype(jnp.bfloat16)
    score_scale = HEAD_DIM ** (-0.5)
    grad_queries = (
        jnp.einsum("hqk,khd->qhd", grad_scores, heads_view[1], preferred_element_type=jnp.float32)
        * score_scale
    )
    grad_keys = (
        jnp.einsum("hqk,qhd->khd", grad_scores, heads_view[0], preferred_element_type=jnp.float32)
        * score_scale
    )
    grad_projected = (
        jnp.stack([grad_queries, grad_keys, grad_values])
        .astype(jnp.bfloat16)
        .reshape(3, length, -1)
    )
    projection_grad = jnp.einsum(
        "td,ste->sde", normed_one, grad_projected, preferred_element_type=jnp.float32
    )
    grad_normed = lax.psum(
        jnp.einsum(
            "ste,sde->td", grad_projected, attention_weight[:3], preferred_element_type=jnp.float32
        ),
        "mp",
    )
    _, pullback = jax.vjp(norm_rows, residual, norm_gains[0], norm_gains[1])
    grad_input, grad_gain, grad_shift = pullback(grad_normed)
    return (
        grad_attention + grad_input,
        jnp.concatenate([projection_grad, output_grad[None]]),
        (grad_gain, grad_shift),
    )


def adam_step(gradient, master, first_old, second_old, step_rate, decay_rate):
    moment = BETA_FIRST * first_old + (1.0 - BETA_FIRST) * gradient
    variance = BETA_SECOND * second_old + (1.0 - BETA_SECOND) * gradient * gradient
    moment_hat = moment / (1.0 - BETA_FIRST**STEP)
    variance_hat = variance / (1.0 - BETA_SECOND**STEP)
    updated = master - step_rate * (
        moment_hat / (jnp.sqrt(variance_hat) + ADAM_EPSILON) + decay_rate * master
    )
    return (moment, variance, updated)


def sum_squares(pieces, model_size):
    squares = jnp.sum(pieces[5] * pieces[5]) / model_size
    for piece_sum in pieces[:5]:
        squares = squares + jnp.sum(piece_sum * piece_sum)
    return squares


def local(
    code_tokens,
    segments,
    layout,
    durations,
    overflow,
    upper_context,
    embed_table,
    condition_weight,
    attention_weight,
    feedforward_weight,
    output_table,
    norm_gains,
    embed_master,
    condition_master,
    attention_master,
    feedforward_master,
    output_master,
    norms_master,
    embed_first,
    condition_first,
    attention_first,
    feedforward_first,
    output_first,
    norms_first,
    embed_second,
    condition_second,
    attention_second,
    feedforward_second,
    output_second,
    norms_second,
):
    model_rank = lax.axis_index("mp")
    model_size = lax.axis_size("mp")
    half_width = embed_table.shape[1]
    keep_flag = 1.0 - overflow[0].astype(jnp.float32)
    local_seconds = keep_flag * jnp.sum(durations.astype(jnp.float32)) / SAMPLE_RATE
    seconds_total = lax.psum(local_seconds, "dp")
    allowed = allowed_mask(segments, layout)
    embedded = jnp.take(embed_table, code_tokens, axis=0).astype(jnp.float32)
    embed_part = contract(upper_context, condition_weight, 1, 1)
    own_columns = (
        lax.dynamic_slice_in_dim(embed_part, model_rank * half_width, half_width, 1) + embedded
    )
    embed_part = lax.dynamic_update_slice_in_dim(
        embed_part, own_columns, model_rank * half_width, 1
    )
    residual = lax.psum(embed_part, "mp")
    after_block, saved_state = layer_forward(
        residual, attention_weight, feedforward_weight, norm_gains, allowed
    )
    loss_local, grad_block, output_grad, norm_three = head_loss(
        after_block, output_table, norm_gains, code_tokens, segments, keep_flag, model_rank
    )
    grad_attention, feedforward_grad, norm_two = feedforward_backward(
        grad_block, saved_state, feedforward_weight, norm_gains
    )
    grad_residual, attention_grad, norm_one = attention_backward(
        grad_attention, saved_state, attention_weight, norm_gains, allowed
    )
    own_grad = lax.dynamic_slice_in_dim(grad_residual, model_rank * half_width, half_width, 1)
    embed_grad = jnp.zeros(embed_table.shape, jnp.float32).at[code_tokens].add(own_grad)
    condition_grad = contract(grad_residual.astype(jnp.bfloat16), upper_context, 0, 0)
    norms_grad = jnp.stack(
        [norm_one[0], norm_one[1], norm_two[0], norm_two[1], norm_three[0], norm_three[1]]
    )
    embed_share, condition_share, attention_share, feedforward_share, output_share, norms_share = (
        lax.psum_scatter(embed_grad, "dp", scatter_dimension=0, tiled=True),
        lax.psum_scatter(condition_grad, "dp", scatter_dimension=0, tiled=True),
        lax.psum_scatter(attention_grad, "dp", scatter_dimension=1, tiled=True),
        lax.psum_scatter(feedforward_grad, "dp", scatter_dimension=1, tiled=True),
        lax.psum_scatter(output_grad, "dp", scatter_dimension=0, tiled=True),
        lax.psum_scatter(norms_grad, "dp", scatter_dimension=1, tiled=True),
    )
    shares = (
        embed_share,
        condition_share,
        attention_share,
        feedforward_share,
        output_share,
        norms_share,
    )
    inverse = 1.0 / seconds_total
    scaled = tuple((piece_sum * inverse for piece_sum in shares))
    squares = sum_squares(scaled, model_size)
    loss_total, square_total = lax.psum((loss_local / model_size, squares), ("dp", "mp"))
    gradient_norm = jnp.sqrt(square_total)
    clip_factor = CLIP_NORM / jnp.maximum(gradient_norm, CLIP_NORM)
    masters = (
        embed_master,
        condition_master,
        attention_master,
        feedforward_master,
        output_master,
        norms_master,
    )
    firsts = (
        embed_first,
        condition_first,
        attention_first,
        feedforward_first,
        output_first,
        norms_first,
    )
    seconds_old = (
        embed_second,
        condition_second,
        attention_second,
        feedforward_second,
        output_second,
        norms_second,
    )
    rates = (RATE_TABLE, RATE_MATRIX, RATE_MATRIX, RATE_MATRIX, RATE_MATRIX, RATE_NORMS)
    decays = (WEIGHT_DECAY, WEIGHT_DECAY, WEIGHT_DECAY, WEIGHT_DECAY, WEIGHT_DECAY, 0.0)
    updates = [
        adam_step(
            scaled[index_slot] * clip_factor,
            masters[index_slot],
            firsts[index_slot],
            seconds_old[index_slot],
            rates[index_slot],
            decays[index_slot],
        )
        for index_slot in range(6)
    ]
    return (
        loss_total,
        seconds_total,
        gradient_norm,
        updates[0][0],
        updates[0][1],
        updates[0][2],
        updates[1][0],
        updates[1][1],
        updates[1][2],
        updates[2][0],
        updates[2][1],
        updates[2][2],
        updates[3][0],
        updates[3][1],
        updates[3][2],
        updates[4][0],
        updates[4][1],
        updates[4][2],
        updates[5][0],
        updates[5][1],
        updates[5][2],
    )


def solution(mesh):
    return jax.shard_map(
        local,
        mesh=mesh,
        in_specs=(
            P("dp"),
            P("dp"),
            P(),
            P("dp"),
            P("dp"),
            P("dp", "mp"),
            P(None, "mp"),
            P(None, "mp"),
            P(None, None, "mp"),
            P(None, None, "mp"),
            P(None, "mp"),
            P(),
            P("dp", "mp"),
            P("dp", "mp"),
            P(None, "dp", "mp"),
            P(None, "dp", "mp"),
            P("dp", "mp"),
            P(None, "dp"),
            P("dp", "mp"),
            P("dp", "mp"),
            P(None, "dp", "mp"),
            P(None, "dp", "mp"),
            P("dp", "mp"),
            P(None, "dp"),
            P("dp", "mp"),
            P("dp", "mp"),
            P(None, "dp", "mp"),
            P(None, "dp", "mp"),
            P("dp", "mp"),
            P(None, "dp"),
        ),
        out_specs=(
            P(),
            P(),
            P(),
            P("dp", "mp"),
            P("dp", "mp"),
            P("dp", "mp"),
            P("dp", "mp"),
            P("dp", "mp"),
            P("dp", "mp"),
            P(None, "dp", "mp"),
            P(None, "dp", "mp"),
            P(None, "dp", "mp"),
            P(None, "dp", "mp"),
            P(None, "dp", "mp"),
            P(None, "dp", "mp"),
            P("dp", "mp"),
            P("dp", "mp"),
            P("dp", "mp"),
            P(None, "dp"),
            P(None, "dp"),
            P(None, "dp"),
        ),
        check_vma=False,
    )
```

profile of v0, /device:TPU:1, one launch (start us, length us, event | category | flops | bytes accessed | tf_op | source)
XLA Modules:
  0.0 2672.2 jit_solution(14923780248671274061)
XLA Ops:
  19.9 73.0 %all-reduce.10.cloned.1.call-done = f32[512,1024]{1,0:T(8,128)} async-done(((f32[512,1024]{1,0:T(8,128)}), f32[512,1024]{1,0:T(8,128)}) %all-reduce.10.cloned.1.call-update) | async-done | bytes 2097168 | tf_op jit(solution)/shard_map/psum | solution.py:275
  111.7 70.3 %all-reduce.12.cloned.1.call-done = f32[512,1024]{1,0:T(8,128)} async-done(((f32[512,1024]{1,0:T(8,128)}), f32[512,1024]{1,0:T(8,128)}) %all-reduce.12.cloned.1.call-update) | async-done | bytes 2097168 | tf_op jit(solution)/shard_map/psum | solution.py:97
  185.8 5.3 fusion.17
  199.9 67.8 %all-reduce.14.cloned.1.call-done = f32[512,1024]{1,0:T(8,128)} async-done(((f32[512,1024]{1,0:T(8,128)}), f32[512,1024]{1,0:T(8,128)}) %all-reduce.14.cloned.1.call-update) | async-done | bytes 2097168 | tf_op jit(solution)/shard_map/psum | solution.py:101
  272.8 4.7 all-gather.5
  277.5 4.7 all-gather.4
  282.2 4.7 all-gather.3
  290.8 73.5 %all-reduce.16.cloned.1.call-done = f32[512,1024]{1,0:T(8,128)} async-done(((f32[512,1024]{1,0:T(8,128)}), f32[512,1024]{1,0:T(8,128)}) %all-reduce.16.cloned.1.call-update) | async-done | bytes 2097168 | tf_op jit(solution)/shard_map/psum | solution.py:135
  367.8 7.7 fusion.8
  380.9 70.3 %all-reduce.18.cloned.1.call-done = f32[512,1024]{1,0:T(8,128)} async-done(((f32[512,1024]{1,0:T(8,128)}), f32[512,1024]{1,0:T(8,128)}) %all-reduce.18.cloned.1.call-update) | async-done | bytes 2097168 | tf_op jit(solution)/shard_map/psum | solution.py:149
  474.5 5.3 fusion.36
  479.9 70.5 %all-reduce.20.cloned.1.call-done = f32[512,1024]{1,0:T(8,128)} async-done(((f32[512,1024]{1,0:T(8,128)}), f32[512,1024]{1,0:T(8,128)}) %all-reduce.20.cloned.1.call-update) | async-done | bytes 2097168 | tf_op jit(solution)/shard_map/psum | solution.py:195
  554.6 6.1 fusion.77
  577.4 10.2 copy.127
  587.7 6.5 scatter_custom_fusion
  601.4 6.5 pad_maximum_fusion
  609.9 139.0 %psum.67 = f32[]{:T(128)} all-reduce(f32[]{:T(128)S(6)} %div.189), channel_id=1, replica_groups=mesh['dp'=64,'mp'=2] {'dp'}, use_global_device_ids=true, to_apply=%region_17.18 | all-reduce | flops 1 | bytes 8 | tf_op jit(solution)/shard_map/psum | solution.py:265
  751.4 81.0 %reduce-scatter.16.cloned.1.call-done = f32[16,6]{1,0:T(8,128)} async-done(((f32[1024,6]{1,0:T(8,128)}), f32[16,6]{1,0:T(8,128)}) %reduce-scatter.16.cloned.1.call-update) | async-done | bytes 400
  834.5 287.5 %reduce-scatter.14.cloned.1.call-done = f32[16,1024]{1,0:T(8,128)} async-done(((f32[1024,1024]{1,0:T(8,128)}), f32[16,1024]{1,0:T(8,128)}) %reduce-scatter.14.cloned.1.call-update) | async-done | bytes 65552 | tf_op jit(solution)/shard_map/reduce_scatter | solution.py:299
  1123.5 283.5 %reduce-scatter.10.cloned.1.call-done = f32[16,512]{1,0:T(8,128)} async-done(((f32[1024,512]{1,0:T(8,128)}), f32[16,512]{1,0:T(8,128)}) %reduce-scatter.10.cloned.1.call-update) | async-done | bytes 32784 | tf_op jit(solution)/shard_map/reduce_scatter | solution.py:296
  1408.5 576.2 %all-reduce.22.cloned.1.call-done = f32[4,1024,512]{2,0,1:T(4,128)} async-done(((f32[4,1024,512]{2,0,1:T(4,128)}), f32[4,1024,512]{2,0,1:T(4,128)}) %all-reduce.22.cloned.1.call-update) | async-done | bytes 8388624
  1986.2 286.3 %reduce-scatter.8.cloned.1.call-done = f32[32,512]{1,0:T(8,128)} async-done(((f32[2048,512]{1,0:T(8,128)}), f32[32,512]{1,0:T(8,128)}) %reduce-scatter.8.cloned.1.call-update) | async-done | bytes 65552 | tf_op jit(solution)/shard_map/reduce_scatter | solution.py:295
  2276.1 308.4 %reduce-scatter.12.cloned.1.call-done = f32[2,16,2048]{2,1,0:T(8,128)} async-done(((f32[2,1024,2048]{2,1,0:T(8,128)}), f32[2,16,2048]{2,1,0:T(8,128)}) %reduce-scatter.12.cloned.1.call-update) | async-done | bytes 262160 | tf_op jit(solution)/shard_map/reduce_scatter | solution.py:298
  2587.4 68.3 %all-reduce.1 = (f32[]{:T(128)}, f32[]{:T(128)}) all-reduce(f32[]{:T(128)S(6)} %div.188, f32[]{:T(128)S(6)} %add.302), channel_id=1, replica_groups=mesh['dp'=64,'mp'=2] {'dp','mp'}, use_global_device_ids=true, to_apply=%region_15.16 | all-reduce | flops 2 | bytes 16 | tf_op jit(solution)/shard_map/psum | solution.py:313
  (237 shorter events, 130.1 us)
Async XLA Ops:
  7.2 85.7 %all-reduce.10.cloned.1.call-start = ((), (), s32[]{:S(2)}) async-start(), calls=%async_computation.5 | async-start | bytes 4194304 | tf_op jit(solution)/shard_map/psum | solution.py:275
  18.6 163.4 %all-reduce.12.cloned.1.call-start = ((), (), s32[]{:S(2)}) async-start(), calls=%async_computation.6 | async-start | bytes 4194304 | tf_op jit(solution)/shard_map/psum | solution.py:97
  111.4 156.3 %all-reduce.14.cloned.1.call-start = ((), (), s32[]{:S(2)}) async-start(), calls=%async_computation.7 | async-start | bytes 4194304 | tf_op jit(solution)/shard_map/psum | solution.py:101
  197.1 167.2 %all-reduce.16.cloned.1.call-start = ((), (), s32[]{:S(2)}) async-start(), calls=%async_computation.8 | async-start | bytes 4194304 | tf_op jit(solution)/shard_map/psum | solution.py:135
  290.4 160.8 %all-reduce.18.cloned.1.call-start = ((), (), s32[]{:S(2)}) async-start(), calls=%async_computation.9 | async-start | bytes 4194304 | tf_op jit(solution)/shard_map/psum | solution.py:149
  380.6 169.8 %all-reduce.20.cloned.1.call-start = ((), (), s32[]{:S(2)}) async-start(), calls=%async_computation.10 | async-start | bytes 4194304 | tf_op jit(solution)/shard_map/psum | solution.py:195
  479.9 352.6 %reduce-scatter.16.cloned.1.call-start = ((), (), s32[]{:S(2)}) async-start(), calls=%async_computation.15 | async-start | bytes 532480
  554.6 567.4 %reduce-scatter.14.cloned.1.call-start = ((), (), s32[]{:S(2)}) async-start(), calls=%async_computation.14 | async-start | bytes 4259840 | tf_op jit(solution)/shard_map/reduce_scatter | solution.py:299
  560.7 846.3 %reduce-scatter.10.cloned.1.call-start = ((), (), s32[]{:S(2)}) async-start(), calls=%async_computation.12 | async-start | bytes 2129920 | tf_op jit(solution)/shard_map/reduce_scatter | solution.py:296
  567.8 1416.9 %all-reduce.22.cloned.1.call-start = ((), (), s32[]{:S(2)}) async-start(), calls=%async_computation.16 | async-start | bytes 16777216
  587.7 1684.9 %reduce-scatter.8.cloned.1.call-start = ((), (), s32[]{:S(2)}) async-start(), calls=%async_computation.11 | async-start | bytes 4259840 | tf_op jit(solution)/shard_map/reduce_scatter | solution.py:295
  594.2 1990.3 %reduce-scatter.12.cloned.1.call-start = ((), (), s32[]{:S(2)}) async-start(), calls=%async_computation.13 | async-start | bytes 17039360 | tf_op jit(solution)/shard_map/reduce_scatter | solution.py:298
  607.9 2048.5 %copy-start.33 = (f32[4,16,512]{2,1,0:T(8,128)S(1)}, f32[4,16,512]{2,1,0:T(8,128)}, u32[]{:S(2)}) copy-start(f32[4,16,512]{2,1,0:T(8,128)} %param.44) | copy-start | bytes 393220
  607.9 2048.6 %copy-start.34 = (f32[4,16,512]{2,1,0:T(8,128)S(1)}, f32[4,16,512]{2,1,0:T(8,128)}, u32[]{:S(2)}) copy-start(f32[4,16,512]{2,1,0:T(8,128)} %param.56) | copy-start | bytes 393220
  607.9 2048.6 %copy-start.35 = (f32[4,16,512]{2,1,0:T(8,128)S(1)}, f32[4,16,512]{2,1,0:T(8,128)}, u32[]{:S(2)}) copy-start(f32[4,16,512]{2,1,0:T(8,128)} %param.50) | copy-start | bytes 393220
  608.0 2049.4 %copy-start.44 = (f32[6,16]{1,0:T(8,128)S(1)}, f32[6,16]{1,0:T(8,128)}, u32[]{:S(2)}) copy-start(f32[6,16]{1,0:T(8,128)} %param.47) | copy-start | bytes 1156
  608.0 2049.4 %copy-start.45 = (f32[6,16]{1,0:T(8,128)S(1)}, f32[6,16]{1,0:T(8,128)}, u32[]{:S(2)}) copy-start(f32[6,16]{1,0:T(8,128)} %param.59) | copy-start | bytes 1156
  608.0 2049.4 %copy-start.46 = (f32[6,16]{1,0:T(8,128)S(1)}, f32[6,16]{1,0:T(8,128)}, u32[]{:S(2)}) copy-start(f32[6,16]{1,0:T(8,128)} %param.53) | copy-start | bytes 1156
  608.6 2051.1 %copy-start.40 = (f32[16,512]{1,0:T(8,128)S(1)}, f32[16,512]{1,0:T(8,128)}, u32[]{:S(2)}) copy-start(f32[16,512]{1,0:T(8,128)} %param.43) | copy-start | bytes 98308
  608.6 2052.5 %copy-start.28 = (f32[2,16,2048]{2,1,0:T(8,128)S(1)}, f32[2,16,2048]{2,1,0:T(8,128)}, u32[]{:S(2)}) copy-start(f32[2,16,2048]{2,1,0:T(8,128)} %param.45) | copy-start | bytes 786436
  608.6 2052.5 %copy-start.29 = (f32[2,16,2048]{2,1,0:T(8,128)S(1)}, f32[2,16,2048]{2,1,0:T(8,128)}, u32[]{:S(2)}) copy-start(f32[2,16,2048]{2,1,0:T(8,128)} %param.57) | copy-start | bytes 786436
  608.6 2052.5 %copy-start.30 = (f32[2,16,2048]{2,1,0:T(8,128)S(1)}, f32[2,16,2048]{2,1,0:T(8,128)}, u32[]{:S(2)}) copy-start(f32[2,16,2048]{2,1,0:T(8,128)} %param.51) | copy-start | bytes 786436
  1407.0 1252.6 %copy-start.32 = (f32[16,512]{1,0:T(8,128)S(1)}, f32[16,512]{1,0:T(8,128)}, u32[]{:S(2)}) copy-start(f32[16,512]{1,0:T(8,128)} %reduce-scatter.10.cloned.1.call-done) | copy-start | bytes 98308
  1408.5 1254.6 %copy-start.31 = (f32[16,1024]{1,0:T(8,128)S(1)}, f32[16,1024]{1,0:T(8,128)}, u32[]{:S(2)}) copy-start(f32[16,1024]{1,0:T(8,128)} %reduce-scatter.14.cloned.1.call-done) | copy-start | bytes 196612
  (47 other events, 1092.4 us)
Sparse Core Ops, SparseCore 0:
  18.7 74.2 all-reduce.9
  111.5 70.3 all-reduce.11
  197.2 70.3 all-reduce.13
  290.5 73.8 all-reduce.15
  380.8 70.3 all-reduce.17
  480.0 70.3 all-reduce.19
  554.7 277.7 reduce-scatter.15
  835.0 287.0 reduce-scatter.13
  1124.4 282.5 reduce-scatter.9
  1409.5 575.1 all-reduce.21
  1987.2 285.3 reduce-scatter.7
  2274.8 309.6 reduce-scatter.11
where the time goes:
time: 2680 us; the launch traced here: 2670 us
  waiting for transfers between devices  2250 us (84%)
  blocking collectives  221 us (8%)
  matrix products  74.2 us (3%)
  other arithmetic  64.9 us (2%)
  local copies, waits for them, and re-layouts  36.7 us (1%)
    unnamed x14, waiting for transfers between devices  657 us
    reduce_scatter x1, waiting for transfers between devices, local(): lax.psum_scatter(feedforward_grad, 'dp', scatter_dimension=1, tiled=True)  308 us
    reduce_scatter x1, waiting for transfers between devices, local(): lax.psum_scatter(output_grad, 'dp', scatter_dimension=0, tiled=True)  288 us
    reduce_scatter x1, waiting for transfers between devices, local(): lax.psum_scatter(embed_grad, 'dp', scatter_dimension=0, tiled=True)  286 us
    reduce_scatter x1, waiting for transfers between devices, local(): lax.psum_scatter(condition_grad, 'dp', scatter_dimension=0, tiled=True)  284 us
    psum x1, blocking collectives, local(): seconds_total = lax.psum(local_seconds, 'dp')  139 us
    psum x1, waiting for transfers between devices, head_loss(): grad_normed = lax.psum(contract(grad_low, output_table, 1, 1), 'mp')  73.5 us
    psum x1, waiting for transfers between devices, local(): residual = lax.psum(embed_part, 'mp')  73 us
  transfers between devices with their start and end apart: 12, of which 12 were waited for; matrix products, arithmetic and copies ran while one was open for 2% of the time, Pallas kernels for 0%

commit v1 on v0

v1 whole, which is shorter than its diff:
```python
import functools

import jax
import jax.numpy as jnp
import numpy as np
from jax import lax
from jax.experimental import pallas as pl
from jax.experimental.pallas import tpu as pltpu
from jax.sharding import Mesh
from jax.sharding import PartitionSpec as P

HEAD_DIM = 64
BLK = 64
CLIPS_DEV = 4
STEP = 10


LAYER_EPS = 1e-05
SAMPLE_RATE = 44100.0
LOG_TWO_NATS = 0.6931471805599453
CLIP_NORM = 1.0
BETA_FIRST = 0.9
BETA_SECOND = 0.95
ADAM_EPSILON = 1e-08
WEIGHT_DECAY = 0.01
RATE_MATRIX = 0.1
RATE_TABLE = 1.0
RATE_NORMS = 1.0
SQUARE_SCALE = 2.0**-9

AXES = ("z", "x", "yl", "c", "yh")
SIZES = (4, 4, 2, 2, 2)
DP = ("z", "x", "yl", "c")
VMEM_LIMIT = 48 * 1024 * 1024
BF16 = jnp.bfloat16
F32 = jnp.float32


def send(value, move):
    pairs = []
    for index in range(int(np.prod(SIZES))):
        z, x, yl, c, yh = (int(i) for i in np.unravel_index(index, SIZES))
        z, x, y, c = move(z, x, yh * 2 + yl, c)
        y %= 4
        pairs.append((index, int(np.ravel_multi_index((z % 4, x % 4, y % 2, c, y // 2), SIZES))))
    return lax.ppermute(value, AXES, pairs)


def swap_core(value):
    return send(value, lambda z, x, y, c: (z, x, y, 1 - c))


def pair_sum(value):
    return value + swap_core(value)


def ring(axis):
    def move(z, x, y, c):
        step = 1 - 2 * c
        return {"z": (z + step, x, y, c), "x": (z, x + step, y, c), "y": (z, x, y + step, c)}[axis]

    return move


def by(axis, count):
    def move(z, x, y, c):
        return {"z": (z + count, x, y, c), "x": (z, x + count, y, c), "y": (z, x, y + count, c)}[axis]

    return move


def flipped(axis, bit):
    def move(z, x, y, c):
        return {"z": (z ^ bit, x, y, c), "x": (z, x ^ bit, y, c), "y": (z, x, y ^ bit, c)}[axis]

    return move


def place_kernel(outer_stride, inner_stride, s_ref, native_ref, b0, b1, b2, b3, out_ref):
    width = native_ref.shape[-1]
    out_ref[0, :, :width] = native_ref[0]
    outer, inner, sign = s_ref[0], s_ref[1], s_ref[2]
    for j, buf in enumerate((b0, b1, b2, b3)):
        outer_at = lax.rem(outer - sign * j + 8, 4)
        for i in range(4):
            inner_at = lax.rem(inner - sign * i + 8, 4)
            row = pl.multiple_of(outer_at * outer_stride + inner_at * inner_stride, 64)
            out_ref[0, pl.ds(row, 64), width:] = buf[i, 0].astype(BF16)


def place(native, first_slot, slots, buffers, scalars, outer_stride, inner_stride):
    rows, width = native.shape[1], native.shape[2] // 2
    block = pl.BlockSpec((4, 1, 64, width), lambda k, s: (0, k, 0, 0))
    return pl.pallas_call(
        functools.partial(place_kernel, outer_stride, inner_stride),
        grid_spec=pltpu.PrefetchScalarGridSpec(
            num_scalar_prefetch=1,
            grid=(slots,),
            in_specs=[pl.BlockSpec((1, rows, width), lambda k, s: (first_slot + k, 0, s[3]))]
            + [block] * 4,
            out_specs=pl.BlockSpec((1, rows, 2 * width), lambda k, s: (k, 0, 0)),
        ),
        out_shape=jax.ShapeDtypeStruct((slots, rows, 2 * width), BF16),
        compiler_params=pltpu.CompilerParams(vmem_limit_bytes=VMEM_LIMIT),
        cost_estimate=pl.CostEstimate(
            flops=0, bytes_accessed=slots * rows * width * 10, transcendentals=0
        ),
    )(scalars, native, *buffers)


def place_halves_kernel(s_ref, native_ref, near_ref, far_ref, out_ref):
    half, width = near_ref.shape
    out_ref[:, :width] = native_ref[...]
    near = s_ref[4]
    out_ref[pl.ds(pl.multiple_of(near * half, 64), half), width:] = near_ref[...].astype(BF16)
    out_ref[pl.ds(pl.multiple_of((1 - near) * half, 64), half), width:] = far_ref[...].astype(BF16)


def place_halves(native, near, far, scalars):
    rows, width = native.shape[0], native.shape[1] // 2
    whole = pl.BlockSpec((rows // 2, width), lambda k, s: (0, 0))
    return pl.pallas_call(
        place_halves_kernel,
        grid_spec=pltpu.PrefetchScalarGridSpec(
            num_scalar_prefetch=1,
            grid=(1,),
            in_specs=[pl.BlockSpec((rows, width), lambda k, s: (0, s[3])), whole, whole],
            out_specs=pl.BlockSpec((rows, 2 * width), lambda k, s: (0, 0)),
        ),
        out_shape=jax.ShapeDtypeStruct((rows, 2 * width), BF16),
        compiler_params=pltpu.CompilerParams(vmem_limit_bytes=VMEM_LIMIT),
        cost_estimate=pl.CostEstimate(
            flops=0, bytes_accessed=rows * width * 10, transcendentals=0
        ),
    )(scalars, native, near, far)


def own_quarter(half, core):
    width = half.shape[-1] // 2
    return jnp.where(core == 0, half[..., :width], half[..., width:])


def row_block(native, core, block):
    slots, rows, width = native.shape
    view = native.reshape(slots, rows // 64, 64, width)
    rows_here = lax.dynamic_slice_in_dim(view, block, 1, 1)[:, 0]
    return own_quarter(rows_here, core).astype(F32)


def gathered(piece, first_axis, second_axis):
    pieces = [piece]
    for _ in range(3):
        pieces.append(send(pieces[-1], ring(first_axis)))
    buffers = [jnp.stack(pieces)]
    for _ in range(3):
        buffers.append(send(buffers[-1], ring(second_axis)))
    return buffers


def chunk_kernel(mode, has_recv, s_ref, lhs_ref, rhs_ref, *rest):
    out_ref = rest[-1]
    rhs = rhs_ref[...].reshape(rhs_ref.shape[-2:])
    rows, width = out_ref.shape[-2:]
    if mode == "hot":
        row_id = lax.broadcasted_iota(jnp.int32, (rows, rhs.shape[0]), 0)
        code = ((row_id // 128) * 4 + s_ref[0]) * 128 + lax.rem(row_id, 128)
        lhs = (code == lhs_ref[...]).astype(F32).astype(BF16)
        high = rhs.astype(BF16)
        low = (rhs - high.astype(F32)).astype(BF16)
        total = jnp.dot(lhs, high, preferred_element_type=F32)
        total += jnp.dot(lhs, low, preferred_element_type=F32)
    else:
        lhs = lhs_ref[...].reshape(rows, lhs_ref.shape[-1])
        total = jnp.dot(lhs, rhs, preferred_element_type=F32)
    total = total.reshape(out_ref.shape)
    if has_recv:
        total += rest[0][...]
    out_ref[...] = total


def chunk_product(order, lhs, rhs, rhs_spec, rows, width, tile, scalars, recv, hot=False):
    tokens = 512
    steps = width // tile
    if hot:
        lhs_spec = pl.BlockSpec((1, tokens), lambda *g: (0, 0))
    elif order == "x":
        lhs = lhs.reshape(4, 4, 64, tokens)
        lhs_spec = pl.BlockSpec((4, 1, 64, tokens), lambda *g: (0, g[-1][0], 0, 0))
    elif order == "z":
        lhs = lhs.reshape(4, 256, tokens)
        lhs_spec = pl.BlockSpec((1, 256, tokens), lambda *g: (g[-1][0], 0, 0))
    else:
        lhs = lhs.reshape(16, 2, 32, tokens)
        lhs_spec = pl.BlockSpec((16, 1, 32, tokens), lambda *g: (0, g[-1][0], 0, 0))
    if order == "y":
        grid = (steps,)
        out_spec = pl.BlockSpec((rows, tile), lambda j, s: (0, j))
        out_shape = jax.ShapeDtypeStruct((rows, width), F32)
        halves = 1
    else:
        grid = (2, steps)
        out_spec = pl.BlockSpec((1, rows, tile), lambda h, j, s: (h, 0, j))
        out_shape = jax.ShapeDtypeStruct((2, rows, width), F32)
        halves = 2
    operands = [lhs, rhs] + ([] if recv is None else [recv])
    in_specs = [lhs_spec, rhs_spec] + ([] if recv is None else [out_spec])
    moved = halves * rows * width * 4
    return pl.pallas_call(
        functools.partial(chunk_kernel, "hot" if hot else "plain", recv is not None),
        grid_spec=pltpu.PrefetchScalarGridSpec(
            num_scalar_prefetch=1, grid=grid, in_specs=in_specs, out_specs=out_spec
        ),
        out_shape=out_shape,
        compiler_params=pltpu.CompilerParams(vmem_limit_bytes=VMEM_LIMIT),
        cost_estimate=pl.CostEstimate(
            flops=2 * tokens * halves * rows * width,
            bytes_accessed=moved * (1 if recv is None else 2),
            transcendentals=0,
        ),
    )(scalars, *operands)


def ring_scatter(axis, place_at, sign, make):
    total = make(lax.rem(place_at - sign + 8, 4), None)
    for k in range(2, 5):
        total = make(lax.rem(place_at - k * sign + 8, 4), send(total, ring(axis)))
    return total


def added(part, arrived):
    return part if arrived is None else part + arrived


class Spot:
    def __init__(self):
        self.z, self.x, self.yl, self.c, self.yh = (lax.axis_index(a) for a in AXES)
        self.y = self.yh * 2 + self.yl
        self.sign = 1 - 2 * self.c


def reduce_rows(order, spot, lhs, rhs, block, rhs_at, width, tile, per_device=16, hot=False):
    pair = 2 * per_device

    def product(chunk, half, arrived):
        scalars = jnp.stack([chunk, half, spot.c, spot.yh]).astype(jnp.int32)
        rows = pair * (16 if order == "y" else 8)
        if order == "y":
            spec = pl.BlockSpec(block, lambda j, s: rhs_at(s[1], j, s))
        else:
            spec = pl.BlockSpec(block, lambda h, j, s: rhs_at(h, j, s))
        return chunk_product(order, lhs, rhs, spec, rows, width, tile, scalars, arrived, hot)

    def half_of(y):
        return lax.rem(y // 2 + spot.yh, 2)

    if order == "x":
        first = ring_scatter("x", spot.x, spot.sign, lambda k, a: product(k, spot.c, a))
        first = first.reshape(2, 4, 2, pair, width)
        second = ring_scatter(
            "y",
            spot.y,
            spot.sign,
            lambda k, a: added(
                lax.dynamic_slice(
                    first, (half_of(k), 0, lax.rem(k, 2), 0, 0), (1, 4, 1, pair, width)
                ).reshape(4, pair, width),
                a,
            ),
        )
        third = ring_scatter(
            "z", spot.z, spot.sign, lambda k, a: added(lax.dynamic_index_in_dim(second, k, 0, False), a)
        )
    elif order == "z":
        first = ring_scatter("z", spot.z, spot.sign, lambda k, a: product(k, spot.c, a))
        first = first.reshape(2, 4, 2, pair, width)
        second = ring_scatter(
            "x", spot.x, spot.sign, lambda k, a: added(lax.dynamic_index_in_dim(first, k, 1, False), a)
        )
        third = ring_scatter(
            "y",
            spot.y,
            spot.sign,
            lambda k, a: added(
                lax.dynamic_slice(
                    second, (half_of(k), lax.rem(k, 2), 0, 0), (1, 1, pair, width)
                ).reshape(pair, width),
                a,
            ),
        )
    else:
        first = ring_scatter(
            "y", spot.y, spot.sign, lambda k, a: product(lax.rem(k, 2), half_of(k), a)
        )
        first = first.reshape(4, 4, pair, width)
        second = ring_scatter(
            "z", spot.z, spot.sign, lambda k, a: added(lax.dynamic_index_in_dim(first, k, 0, False), a)
        )
        third = ring_scatter(
            "x", spot.x, spot.sign, lambda k, a: added(lax.dynamic_index_in_dim(second, k, 0, False), a)
        )
    return third


def sum_of_four(value, axis, place_at):
    pieces = [value] + [send(value, by(axis, k)) for k in (1, 2, 3)]
    total = None
    for at in range(4):
        back = lax.rem(place_at - at + 4, 4)
        part = pieces[3]
        for k in (2, 1, 0):
            part = jnp.where(back == k, pieces[k], part)
        total = part if total is None else total + part
    return total


def contract(left_side, right_side, left_dim, right_dim):
    return lax.dot_general(
        left_side,
        right_side,
        (((left_dim,), (right_dim,)), ((), ())),
        preferred_element_type=jnp.float32,
    )


def norm_rows(values, gain_row, shift_row):
    average = jnp.mean(values, axis=-1, keepdims=True)
    centred = values - average
    variance = jnp.mean(centred * centred, axis=-1, keepdims=True)
    return centred * lax.rsqrt(variance + LAYER_EPS) * gain_row + shift_row


def allowed_mask(segments, layout):
    length = segments.shape[0]
    position = jnp.arange(length)
    blocks = layout.shape[0]
    block_open = (
        jnp.broadcast_to(layout[:, None, :, None], (blocks, BLK, blocks, BLK)).reshape(
            length, length
        )
        > 0
    )
    causal = position[None, :] <= position[:, None]
    return causal & (segments[:, None] == segments[None, :]) & block_open


def masked_scores(queries, keys_low, allowed):
    scores = jnp.einsum(
        "qhd,khd->hqk", queries, keys_low, preferred_element_type=jnp.float32
    ) * HEAD_DIM ** (-0.5)
    return jnp.where(allowed[None], scores, -1e30)


def layer_forward(residual, project_weight, mix_weight, up_weight, down_weight, norm_gains, allowed):
    length = residual.shape[0]
    heads_local = project_weight.shape[2] // HEAD_DIM
    normed_one = norm_rows(residual, norm_gains[0], norm_gains[1]).astype(jnp.bfloat16)
    projected = jnp.einsum(
        "td,sde->ste", normed_one, project_weight, preferred_element_type=jnp.float32
    ).astype(jnp.bfloat16)
    heads_view = projected.reshape(3, length, heads_local, HEAD_DIM)
    masked = masked_scores(heads_view[0], heads_view[1], allowed)
    row_top = jnp.max(masked, axis=-1, keepdims=True)
    exponents = jnp.exp(masked - row_top)
    row_sums = jnp.sum(exponents, axis=-1, keepdims=True)
    attend_low = (exponents / row_sums).astype(jnp.bfloat16)
    log_total = row_top + jnp.log(row_sums)
    mixed_low = (
        jnp.einsum("hqk,khd->qhd", attend_low, heads_view[2], preferred_element_type=jnp.float32)
        .astype(jnp.bfloat16)
        .reshape(length, -1)
    )
    after_attention = residual + pair_sum(contract(mixed_low, mix_weight, 1, 1))
    normed_two = norm_rows(after_attention, norm_gains[2], norm_gains[3]).astype(jnp.bfloat16)
    pre_act = jnp.dot(normed_two, up_weight, preferred_element_type=jnp.float32)
    activated = jax.nn.gelu(pre_act).astype(jnp.bfloat16)
    after_block = after_attention + pair_sum(contract(activated, down_weight, 1, 1))
    saved_state = (
        residual,
        normed_one,
        heads_view,
        log_total,
        mixed_low,
        after_attention,
        normed_two,
        pre_act,
        activated,
    )
    return (after_block, saved_state)


def head_loss(after_block, output_table, norm_gains, code_tokens, segments, keep_flag, spot):
    normed_three = norm_rows(after_block, norm_gains[4], norm_gains[5]).astype(jnp.bfloat16)
    logits = jnp.dot(normed_three, output_table, preferred_element_type=jnp.float32)
    width = output_table.shape[1]
    quarter = width // 2
    targets = jnp.concatenate([code_tokens[1:], code_tokens[-1:]])
    column = jnp.arange(width)
    code = jnp.where(
        column < quarter,
        spot.yh * width + spot.c * quarter + column,
        (1 - spot.yh) * width + spot.c * quarter + column - quarter,
    )
    target_hit = code[None, :] == targets[:, None]
    row_top = jnp.max(logits, axis=1)
    row_sums = jnp.sum(jnp.exp(logits - row_top[:, None]), axis=1)
    picked = jnp.sum(jnp.where(target_hit, logits, 0.0), axis=1)
    other = swap_core(jnp.stack([row_top, row_sums, picked]))
    both_top = jnp.maximum(row_top, other[0])
    both_sums = row_sums * jnp.exp(row_top - both_top) + other[1] * jnp.exp(other[0] - both_top)
    log_norm = both_top + jnp.log(both_sums)
    next_segment = jnp.concatenate([segments[1:], jnp.full((1,), -1, jnp.int32)])
    counted = ((segments == next_segment) & (segments < CLIPS_DEV)).astype(jnp.float32) * keep_flag
    loss_local = jnp.sum(counted * (log_norm - (picked + other[2]))) / LOG_TWO_NATS
    grad_logits = (counted / LOG_TWO_NATS)[:, None] * (
        jnp.exp(logits - log_norm[:, None]) - target_hit.astype(jnp.float32)
    )
    grad_low = grad_logits.astype(jnp.bfloat16)
    grad_normed = pair_sum(contract(grad_low, output_table, 1, 1))
    _, pullback = jax.vjp(norm_rows, after_block, norm_gains[4], norm_gains[5])
    grad_input, grad_gain, grad_shift = pullback(grad_normed)
    return (loss_local, grad_input, normed_three, grad_low, (grad_gain, grad_shift))


def feedforward_backward(grad_block, saved_state, up_weight, down_weight, norm_gains):
    after_attention, normed_two, pre_act, activated = saved_state[5:]
    branch_low = grad_block.astype(jnp.bfloat16)
    grad_activated = jnp.dot(branch_low, down_weight, preferred_element_type=jnp.float32)
    _, gelu_pull = jax.vjp(jax.nn.gelu, pre_act)
    grad_pre = gelu_pull(grad_activated)[0].astype(jnp.bfloat16)
    grad_normed = pair_sum(contract(grad_pre, up_weight, 1, 1))
    _, pullback = jax.vjp(norm_rows, after_attention, norm_gains[2], norm_gains[3])
    grad_input, grad_gain, grad_shift = pullback(grad_normed)
    return (grad_block + grad_input, branch_low, grad_pre, (grad_gain, grad_shift))


def attention_backward(grad_attention, saved_state, project_weight, mix_weight, norm_gains, allowed):
    residual, normed_one, heads_view, log_total, mixed_low = saved_state[:5]
    length = residual.shape[0]
    heads_local = heads_view.shape[2]
    branch_low = grad_attention.astype(jnp.bfloat16)
    grad_mixed = (
        jnp.dot(branch_low, mix_weight, preferred_element_type=jnp.float32)
        .astype(jnp.bfloat16)
        .reshape(length, heads_local, HEAD_DIM)
    )
    masked = masked_scores(heads_view[0], heads_view[1], allowed)
    attend_full = jnp.exp(masked - log_total)
    attend_low = attend_full.astype(jnp.bfloat16)
    grad_values = jnp.einsum(
        "hqk,qhd->khd", attend_low, grad_mixed, preferred_element_type=jnp.float32
    )
    grad_attend = jnp.einsum(
        "qhd,khd->hqk", grad_mixed, heads_view[2], preferred_element_type=jnp.float32
    )
    grad_scores = (
        attend_full * (grad_attend - jnp.sum(attend_full * grad_attend, axis=-1, keepdims=True))
    ).astype(jnp.bfloat16)
    score_scale = HEAD_DIM ** (-0.5)
    grad_queries = (
        jnp.einsum("hqk,khd->qhd", grad_scores, heads_view[1], preferred_element_type=jnp.float32)
        * score_scale
    )
    grad_keys = (
        jnp.einsum("hqk,qhd->khd", grad_scores, heads_view[0], preferred_element_type=jnp.float32)
        * score_scale
    )
    grad_projected = (
        jnp.stack([grad_queries, grad_keys, grad_values])
        .astype(jnp.bfloat16)
        .reshape(3, length, -1)
    )
    grad_normed = pair_sum(
        jnp.einsum(
            "ste,sde->td", grad_projected, project_weight, preferred_element_type=jnp.float32
        )
    )
    _, pullback = jax.vjp(norm_rows, residual, norm_gains[0], norm_gains[1])
    grad_input, grad_gain, grad_shift = pullback(grad_normed)
    return (grad_attention + grad_input, branch_low, grad_projected, (grad_gain, grad_shift))


def adam_step(gradient, master, first_old, second_old, step_rate, decay_rate):
    moment = BETA_FIRST * first_old + (1.0 - BETA_FIRST) * gradient
    variance = BETA_SECOND * second_old + (1.0 - BETA_SECOND) * gradient * gradient
    moment_hat = moment / (1.0 - BETA_FIRST**STEP)
    variance_hat = variance / (1.0 - BETA_SECOND**STEP)
    updated = master - step_rate * (
        moment_hat / (jnp.sqrt(variance_hat) + ADAM_EPSILON) + decay_rate * master
    )
    return (moment, variance, updated)


def local(
    code_tokens,
    segments,
    layout,
    durations,
    overflow,
    upper_context,
    embed_table,
    condition_weight,
    attention_weight,
    feedforward_weight,
    output_table,
    norm_gains,
    embed_master,
    condition_master,
    attention_master,
    feedforward_master,
    output_master,
    norms_master,
    embed_first,
    condition_first,
    attention_first,
    feedforward_first,
    output_first,
    norms_first,
    embed_second,
    condition_second,
    attention_second,
    feedforward_second,
    output_second,
    norms_second,
):
    spot = Spot()
    core, yh = spot.c, spot.yh
    settled = core == yh
    length = code_tokens.shape[0]

    keep_native = 1.0 - overflow[0].astype(jnp.float32)
    local_seconds = keep_native * jnp.sum(durations.astype(jnp.float32)) / SAMPLE_RATE
    native_ints = jnp.concatenate([code_tokens, segments, jnp.broadcast_to(overflow, (128,))])
    window_ints = jnp.where(settled, native_ints, swap_core(native_ints))
    window_tokens = window_ints[:length]
    window_segments = window_ints[length : 2 * length]
    keep_flag = 1.0 - window_ints[2 * length].astype(jnp.float32)

    embedded = jnp.take(embed_table, code_tokens, axis=0)
    width = embed_table.shape[1] // 2
    own_part = jnp.concatenate(
        [own_quarter(upper_context, core), own_quarter(embedded, core)], axis=1
    ).astype(F32)
    sibling_part = jnp.concatenate(
        [own_quarter(upper_context, 1 - core), own_quarter(embedded, 1 - core)], axis=1
    ).astype(F32)
    arrived_part = lax.optimization_barrier(swap_core(sibling_part))
    near_part = jnp.where(settled, own_part, arrived_part)
    far_part = lax.optimization_barrier(
        send(jnp.where(settled, arrived_part, own_part), by("y", 2))
    )
    context = jnp.concatenate([near_part[:, :width], far_part[:, :width]], axis=1).astype(BF16)

    block = spot.z * 4 + spot.x

    def crossed(value):
        return send(value, lambda z, x, y, c: (z, x, 3 - y, c))

    condition_three = condition_weight[None]
    piece_small = jnp.concatenate(
        [
            row_block(condition_three, core, block),
            row_block(attention_weight, core, block)[3:],
        ]
    )
    piece_project = row_block(attention_weight, core, block)[:3]
    piece_up = row_block(feedforward_weight, core, block)[:1]
    piece_down = row_block(feedforward_weight, core, block)[1:]
    buffers_small = gathered(crossed(piece_small), "z", "x")
    buffers_project = gathered(crossed(piece_project), "x", "z")
    buffers_up = gathered(crossed(piece_up), "x", "z")
    buffers_down = gathered(crossed(piece_down), "z", "x")
    scalars_xz = jnp.stack([spot.z, spot.x, spot.sign, core, spot.yl]).astype(jnp.int32)
    scalars_zx = jnp.stack([spot.x, spot.z, spot.sign, core, spot.yl]).astype(jnp.int32)
    condition_full = place(
        condition_three, 0, 1, [b[:, :1] for b in buffers_small], scalars_zx, 64, 256
    )[0]
    mix_full = place(attention_weight, 3, 1, [b[:, 1:] for b in buffers_small], scalars_zx, 64, 256)[0]
    project_full = place(attention_weight, 0, 3, buffers_project, scalars_xz, 256, 64)
    up_full = place(feedforward_weight, 0, 1, buffers_up, scalars_xz, 256, 64)[0]
    down_full = place(feedforward_weight, 1, 1, buffers_down, scalars_zx, 64, 256)[0]
    table_halves = own_quarter(output_table, core).reshape(2, output_table.shape[0] // 2, -1)
    near_half = crossed(lax.dynamic_index_in_dim(table_halves, 1 - spot.yl, 0, False).astype(F32))
    far_half = send(near_half, flipped("y", 1))
    output_full = place_halves(output_table, near_half, far_half, scalars_xz)

    allowed = allowed_mask(window_segments, layout)
    near_slot, far_slot = yh * 2 + core, (1 - yh) * 2 + core
    embed_part = contract(context, condition_full, 1, 1)
    columns = []
    for slot in range(4):
        columns.append(
            embed_part[:, slot * width : (slot + 1) * width]
            + jnp.where(
                near_slot == slot,
                near_part[:, width:],
                jnp.where(far_slot == slot, far_part[:, width:], 0.0),
            )
        )
    residual = pair_sum(jnp.concatenate(columns, axis=1))

    after_block, saved_state = layer_forward(
        residual, project_full, mix_full, up_full, down_full, norm_gains, allowed
    )
    loss_local, grad_block, normed_three, grad_logits, norm_three = head_loss(
        after_block, output_full, norm_gains, window_tokens, window_segments, keep_flag, spot
    )
    output_sum = reduce_rows(
        "y", spot, normed_three.T, grad_logits, (length, 512), lambda h, j, s: (0, h), 512, 512
    )
    grad_attention, down_left, grad_pre, norm_two = feedforward_backward(
        grad_block, saved_state, up_full, down_full, norm_gains
    )
    down_sum = reduce_rows(
        "z", spot, down_left.T, saved_state[8], (length, 512), lambda h, j, s: (0, h * 2 + j), 1024, 512
    )
    up_sum = reduce_rows(
        "x", spot, saved_state[6].T, grad_pre, (length, 512), lambda h, j, s: (0, h * 2 + j), 1024, 512
    )
    grad_residual, mix_left, grad_projected, norm_one = attention_backward(
        grad_attention, saved_state, project_full, mix_full, norm_gains, allowed
    )
    mix_sum = reduce_rows(
        "z", spot, mix_left.T, saved_state[4], (length, 256), lambda h, j, s: (0, h), 256, 256
    )
    project_sum = reduce_rows(
        "y", spot, saved_state[1].T, grad_projected, (1, length, 256), lambda h, j, s: (j, 0, h), 768, 256
    )
    condition_sum = reduce_rows(
        "z", spot, grad_residual.astype(BF16).T, context, (length, 256), lambda h, j, s: (0, h), 256, 256
    )
    embed_sum = reduce_rows(
        "x",
        spot,
        window_tokens[None],
        grad_residual,
        (length, 256),
        lambda h, j, s: (0, lax.rem(s[3] + h, 2) * 2 + s[2]),
        256,
        256,
        per_device=32,
        hot=True,
    )
    norms_grad = jnp.stack(
        [norm_one[0], norm_one[1], norm_two[0], norm_two[1], norm_three[0], norm_three[1]]
    )
    for axis in ("x", "y", "z"):
        for bit in (1, 2):
            norms_grad = norms_grad + send(norms_grad, flipped(axis, bit))
    dp_rank = ((spot.z * 4 + spot.x) * 2 + spot.yl) * 2 + core
    norms_share = lax.dynamic_slice_in_dim(norms_grad, dp_rank * 16, 16, 1)

    sums = [output_sum, down_sum, up_sum, mix_sum, project_sum, condition_sum, embed_sum]
    squares = 0.5 * jnp.sum((norms_share * SQUARE_SCALE) ** 2)
    for piece in sums:
        squares = squares + jnp.sum((piece * SQUARE_SCALE) ** 2)
    scalars = jnp.stack([0.5 * loss_local, squares, 0.5 * local_seconds])
    scalars = pair_sum(jnp.broadcast_to(scalars[:, None], (3, 128)))
    for axis, at in (("x", spot.x), ("z", spot.z), ("y", spot.y)):
        scalars = sum_of_four(scalars, axis, at)
    loss_total, seconds_total = scalars[0, 0], scalars[2, 0]
    inverse = 1.0 / seconds_total
    gradient_norm = jnp.sqrt(scalars[1, 0]) * (inverse / SQUARE_SCALE)
    clip_factor = CLIP_NORM / jnp.maximum(gradient_norm, CLIP_NORM)

    flat = [piece.reshape(2, 16, -1) for piece in sums[:-1]] + [sums[-1].reshape(2, 16, 512)]
    flat = jnp.concatenate(flat, axis=2)
    mine = lax.dynamic_index_in_dim(flat, core, 0, False)
    theirs = swap_core(lax.dynamic_index_in_dim(flat, 1 - core, 0, False))
    low_side = jnp.where(core == 0, mine, theirs)
    high_side = jnp.where(core == 0, theirs, mine)

    def share(start, stop):
        return low_side[:, start:stop], high_side[:, start:stop]

    output_share = jnp.concatenate(share(0, 512), axis=1)
    feedforward_share = jnp.stack(
        [jnp.concatenate(share(1536, 2560), axis=1), jnp.concatenate(share(512, 1536), axis=1)]
    )
    mix_low, mix_high = share(2560, 2816)
    project_low, project_high = share(2816, 3584)
    attention_share = jnp.stack(
        [
            jnp.concatenate(
                [project_low[:, 256 * k : 256 * k + 256], project_high[:, 256 * k : 256 * k + 256]],
                axis=1,
            )
            for k in range(3)
        ]
        + [jnp.concatenate([mix_low, mix_high], axis=1)]
    )
    condition_share = jnp.concatenate(share(3584, 3840), axis=1)
    embed_share = jnp.concatenate([part.reshape(32, 256) for part in share(3840, 4352)], axis=1)

    shares = (
        embed_share,
        condition_share,
        attention_share,
        feedforward_share,
        output_share,
        norms_share,
    )
    masters = (
        embed_master,
        condition_master,
        attention_master,
        feedforward_master,
        output_master,
        norms_master,
    )
    firsts = (
        embed_first,
        condition_first,
        attention_first,
        feedforward_first,
        output_first,
        norms_first,
    )
    seconds_old = (
        embed_second,
        condition_second,
        attention_second,
        feedforward_second,
        output_second,
        norms_second,
    )
    rates = (RATE_TABLE, RATE_MATRIX, RATE_MATRIX, RATE_MATRIX, RATE_MATRIX, RATE_NORMS)
    decays = (WEIGHT_DECAY, WEIGHT_DECAY, WEIGHT_DECAY, WEIGHT_DECAY, WEIGHT_DECAY, 0.0)
    outputs = [loss_total, seconds_total, gradient_norm]
    for slot in range(6):
        outputs += adam_step(
            shares[slot] * inverse * clip_factor,
            masters[slot],
            firsts[slot],
            seconds_old[slot],
            rates[slot],
            decays[slot],
        )
    return tuple(outputs)


def solution(mesh):
    torus = Mesh(mesh.devices.reshape(SIZES), AXES)
    table, slotted = P(DP, "yh"), P(None, DP, "yh")
    state = (table, table, slotted, slotted, table, P(None, DP))
    results = tuple(spec for spec in state for _ in range(3))
    return jax.shard_map(
        local,
        mesh=torus,
        in_specs=(
            P(DP),
            P(DP),
            P(),
            P(DP),
            P(DP),
            table,
            P(None, "yh"),
            P(None, "yh"),
            P(None, None, "yh"),
            P(None, None, "yh"),
            P(None, "yh"),
            P(),
        )
        + state * 3,
        out_specs=(P(), P(), P()) + results,
        check_vma=False,
    )
```

time: 2680 us -> 697 us (0.26)
  waiting for transfers between devices: 2250 us -> 187 us
  blocking collectives: 221 us -> 0 us
  starting transfers between devices: 1.75 us -> 178 us
  Pallas kernels: 0 us -> 102 us
  local copies, waits for them, and re-layouts: 36.7 us -> 67.7 us
  matrix products: 74.2 us -> 46.5 us
    reduce_scatter x4 -> x0, waiting for transfers between devices: 1170 us -> none  [the longest x1 308 us: local(): lax.psum_scatter(feedforward_grad, 'dp', scatter_dimension=1, tiled=True)]
    unnamed x14 -> x0, waiting for transfers between devices: 657 us -> none
    psum x6 -> x0, waiting for transfers between devices: 425 us -> none  [the longest x1 73.5 us: head_loss(): grad_normed = lax.psum(contract(grad_low, output_table, 1, 1), 'mp')]
    psum x2 -> x0, blocking collectives: 207 us -> none  [the longest x1 139 us: local(): seconds_total = lax.psum(local_seconds, 'dp')]
    ppermute x0 -> x120, waiting for transfers between devices: none -> 187 us  [send(): return lax.ppermute(value, AXES, pairs)]
    ppermute x0 -> x120, starting transfers between devices: none -> 178 us  [send(): return lax.ppermute(value, AXES, pairs)]
    pallas_call x0 -> x34, Pallas kernels: none -> 102 us  [the longest x28 81.7 us: chunk_product(): pl.pallas_call(functools.partial(chunk_kernel, 'hot' if hot else 'plain',...]
  transfers between devices with their start and end apart: 12 -> 120, of which waited for: 12 -> 44; matrix products, arithmetic and copies ran while one was open for 2% -> 21% of each run, Pallas kernels for 0% -> 15%
where the time goes in v1:
time: 697 us; the launch traced here: 684 us
  waiting for transfers between devices  187 us (27%)
  starting transfers between devices  178 us (26%)
  Pallas kernels  102 us (15%)
  other arithmetic  88.2 us (13%)
  local copies, waits for them, and re-layouts  67.7 us (10%)
  matrix products  46.5 us (7%)
  between operations  13.8 us (2%)
    ppermute x120, waiting for transfers between devices, send(): return lax.ppermute(value, AXES, pairs)  187 us
    ppermute x120, starting transfers between devices, send(): return lax.ppermute(value, AXES, pairs)  178 us
    pallas_call x28, Pallas kernels, chunk_product(): pl.pallas_call(functools.partial(chunk_kernel, 'hot' if hot else 'plain',...  81.7 us
    unnamed x258, local copies, waits for them, and re-layouts  29.7 us
    pallas_call x5, Pallas kernels, place(): pl.pallas_call(functools.partial(place_kernel, outer_stride, inner_stride...  18 us
    add x35, other arithmetic, added(): return part if arrived is None else part + arrived  16 us
  transfers between devices with their start and end apart: 120, of which 44 were waited for; matrix products, arithmetic and copies ran while one was open for 21% of the time, Pallas kernels for 15%

profile of v1, /device:TPU:1, one launch (start us, length us, event | category | flops | bytes accessed | tf_op | source)
XLA Modules:
  0.0 683.8 jit_solution(1995769118229755563)
XLA Ops:
  61.0 4.5 collective-permute-done.2
  73.8 5.7 collective-permute-start.10
  124.0 4.9 shard_map.446
  151.9 6.9 %collective-permute-done.25.b3 = f32[4,1,64,1024]{3,2,1,0:T(8,128)S(1)} collective-permute-done((f32[4,1,64,1024]{3,2,1,0:T(8,128)}, f32[4,1,64,1024]{3,2,1,0:T(8,128)S(1)}, u32[]{:S(2)}, u32[]{:S(2)}) %collective-permute-start.25) | collective-permute-done | bytes 1048608 | tf_op jit(solution)/shard_map/ppermute | solution.py:46
  161.0 5.1 shard_map.448
  166.1 5.7 shard_map.449
  175.3 4.9 multiply_convert_fusion.1
  187.3 23.5 %collective-permute-done.35.far_ref = f32[512,512]{1,0:T(8,128)} collective-permute-done((f32[512,512]{1,0:T(8,128)S(1)}, f32[512,512]{1,0:T(8,128)}, u32[]{:S(2)}, u32[]{:S(2)}) %collective-permute-start.35) | collective-permute-done | bytes 1048608 | tf_op jit(solution)/shard_map/ppermute | solution.py:46
  228.5 4.3 multiply_reduce_fusion.2
  242.1 7.6 %fusion.8.rhs_ref = bf16[512,2048]{1,0:T(8,128)(2,1)S(1)} fusion(f32[512,2048]{1,0:T(8,128)} %get-tuple-element.155, bf16[1,1024,2048]{2,1,0:T(8,128)(2,1)} %shard_map.449, f32[512,1024]{1,0:T(8,128)S(1)} %copy-done.70, f32[512]{0:T(512)S(1)} %negate_multiply_fusion.2), kind=kOutput, calls=%fused_computation.17 | convolution fusion | flops 2169503744 | bytes 12584960 | tf_op jit(solution)/shard_map/dot_general | solution.py:427
  264.0 9.8 %collective-permute-done.47.rest_0_ = f32[512,512]{1,0:T(8,128)} collective-permute-done((f32[512,512]{1,0:T(8,128)}, f32[512,512]{1,0:T(8,128)}, u32[]{:S(2)}, u32[]{:S(2)}) %collective-permute-start.47) | collective-permute-done | bytes 1048608 | tf_op jit(solution)/shard_map/ppermute | solution.py:46
  315.3 5.7 convolution_bitcast_fusion
  360.6 20.1 %collective-permute-done.76 = f32[2,2,32,256]{3,2,1,0:T(8,128)S(1)} collective-permute-done((f32[2,2,32,256]{3,2,1,0:T(8,128)S(1)}, f32[2,2,32,256]{3,2,1,0:T(8,128)S(1)}, u32[]{:S(2)}, u32[]{:S(2)}) %collective-permute-start.76) | collective-permute-done | bytes 131104 | tf_op jit(solution)/shard_map/ppermute | solution.py:46
  404.5 9.0 %collective-permute-done.78 = f32[2,2,32,256]{3,2,1,0:T(8,128)S(1)} collective-permute-done((f32[2,2,32,256]{3,2,1,0:T(8,128)S(1)}, f32[2,2,32,256]{3,2,1,0:T(8,128)S(1)}, u32[]{:S(2)}, u32[]{:S(2)}) %collective-permute-start.78) | collective-permute-done | bytes 131104 | tf_op jit(solution)/shard_map/ppermute | solution.py:46
  419.0 5.0 shard_map.456
  457.9 10.9 %collective-permute-done.42 = f32[6,1024]{1,0:T(8,128)S(1)} collective-permute-done((f32[6,1024]{1,0:T(8,128)S(1)}, f32[6,1024]{1,0:T(8,128)S(1)}, u32[]{:S(2)}, u32[]{:S(2)}) %collective-permute-start.42) | collective-permute-done | bytes 24608 | tf_op jit(solution)/shard_map/ppermute | solution.py:46
  472.3 22.5 %collective-permute-done.54 = f32[32,512]{1,0:T(8,128)S(1)} collective-permute-done((f32[32,512]{1,0:T(8,128)S(1)}, f32[32,512]{1,0:T(8,128)S(1)}, u32[]{:S(2)}, u32[]{:S(2)}) %collective-permute-start.54) | collective-permute-done | bytes 65568 | tf_op jit(solution)/shard_map/ppermute | solution.py:46
  512.4 4.3 shard_map.468
  519.6 5.0 shard_map.457
  529.8 5.0 shard_map.461
  535.8 4.2 collective-permute-done.103
  561.9 13.6 %collective-permute-done.99 = f32[32,256]{1,0:T(8,128)S(1)} collective-permute-done((f32[32,256]{1,0:T(8,128)S(1)}, f32[32,256]{1,0:T(8,128)S(1)}, u32[]{:S(2)}, u32[]{:S(2)}) %collective-permute-start.99) | collective-permute-done | bytes 32800 | tf_op jit(solution)/shard_map/ppermute | solution.py:46
  631.5 20.1 %collective-permute-start.109 = (f32[3,128]{1,0:T(4,128)S(1)}, f32[3,128]{1,0:T(4,128)S(1)}, u32[]{:S(2)}, u32[]{:S(2)}) collective-permute-start(f32[3,128]{1,0:T(4,128)S(1)} %broadcast_in_dim.126), channel_id=1, source_target_pairs={{0,2},{1,3},{2,0},{3,1},{4,6},{5,7},{6,4},{7,5},{8,10},{9,11},{10,... | collective-permute-start | bytes 4616 | tf_op jit(solution)/shard_map/ppermute | solution.py:46
  667.5 4.5 collective-permute-start.119
  (730 shorter events, 457.1 us)
Async XLA Ops:
  44.5 35.0 %collective-permute-start.26 = (f32[1,64,1024]{2,1,0:T(8,128)}, f32[1,64,1024]{2,1,0:T(8,128)}, u32[]{:S(2)}, u32[]{:S(2)}) collective-permute-start(f32[1,64,1024]{2,1,0:T(8,128)} %get-tuple-element.102), channel_id=1, source_target_pairs={{0,5},{1,4},{2,7},{3,6},{4,1},{5,0},{6,3},{7,2},{8,13},{9,12},{10,... | collective-permute-start | bytes 786440 | tf_op jit(solution)/shard_map/ppermute | solution.py:46
  45.8 37.0 %collective-permute-start.20 = (f32[1,64,1024]{2,1,0:T(8,128)}, f32[1,64,1024]{2,1,0:T(8,128)S(1)}, u32[]{:S(2)}, u32[]{:S(2)}) collective-permute-start(f32[1,64,1024]{2,1,0:T(8,128)} %collective-permute-done.19), channel_id=1, source_target_pairs={{0,8},{1,9},{2,26},{3,27},{4,12},{5,13},{6,30},{7,31},{8,16},{9,17... | collective-permute-start | bytes 786440 | tf_op jit(solution)/shard_map/ppermute | solution.py:46
  54.7 35.0 %collective-permute-start.15 = (f32[4,3,64,256]{3,2,1,0:T(8,128)S(1)}, f32[4,3,64,256]{3,2,1,0:T(8,128)S(1)}, u32[]{:S(2)}, u32[]{:S(2)}) collective-permute-start(f32[4,3,64,256]{3,2,1,0:T(8,128)S(1)} %pad_maximum_fusion.4.b0), channel_id=1, source_target_pairs={{0,32},{1,33},{2,98},{3,99},{4,36},{5,37},{6,102},{7,103},{8,40},{... | collective-permute-start | bytes 2359304 | tf_op jit(solution)/shard_map/ppermute | solution.py:46
  73.8 55.2 %collective-permute-start.10 = (f32[512,1024]{1,0:T(8,128)}, f32[512,1024]{1,0:T(8,128)}, u32[]{:S(2)}, u32[]{:S(2)}) collective-permute-start(f32[512,1024]{1,0:T(8,128)} %pad_maximum_fusion), channel_id=1, source_target_pairs={{0,2},{1,3},{2,0},{3,1},{4,6},{5,7},{6,4},{7,5},{8,10},{9,11},{10,... | collective-permute-start | bytes 6291464 | tf_op jit(solution)/shard_map/ppermute | solution.py:46
  142.3 29.6 %collective-permute-start.18 = (f32[512,1024]{1,0:T(8,128)}, f32[512,1024]{1,0:T(8,128)}, u32[]{:S(2)}, u32[]{:S(2)}) collective-permute-start(f32[512,1024]{1,0:T(8,128)} %fusion.35), channel_id=1, source_target_pairs={{0,2},{1,3},{2,0},{3,1},{4,6},{5,7},{6,4},{7,5},{8,10},{9,11},{10,... | collective-permute-start | bytes 6291464 | tf_op jit(solution)/shard_map/ppermute | solution.py:46
  149.8 36.2 %collective-permute-start.34 = (f32[512,512]{1,0:T(8,128)}, f32[512,512]{1,0:T(8,128)S(1)}, u32[]{:S(2)}, u32[]{:S(2)}) collective-permute-start(f32[512,512]{1,0:T(8,128)} %bitcast_convert_fusion), channel_id=1, source_target_pairs={{0,5},{1,4},{2,7},{3,6},{4,1},{5,0},{6,3},{7,2},{8,13},{9,12},{10,... | collective-permute-start | bytes 3145736 | tf_op jit(solution)/shard_map/ppermute | solution.py:46
  183.9 29.2 %collective-permute-start.33 = (f32[512,1024]{1,0:T(8,128)}, f32[512,1024]{1,0:T(8,128)}, u32[]{:S(2)}, u32[]{:S(2)}) collective-permute-start(f32[512,1024]{1,0:T(8,128)} %fusion.13), channel_id=1, source_target_pairs={{0,2},{1,3},{2,0},{3,1},{4,6},{5,7},{6,4},{7,5},{8,10},{9,11},{10,... | collective-permute-start | bytes 6291464 | tf_op jit(solution)/shard_map/ppermute | solution.py:46
  253.5 28.2 %collective-permute-start.38 = (f32[512,1024]{1,0:T(8,128)}, f32[512,1024]{1,0:T(8,128)}, u32[]{:S(2)}, u32[]{:S(2)}) collective-permute-start(f32[512,1024]{1,0:T(8,128)} %fusion.15), channel_id=1, source_target_pairs={{0,2},{1,3},{2,0},{3,1},{4,6},{5,7},{6,4},{7,5},{8,10},{9,11},{10,... | collective-permute-start | bytes 6291464 | tf_op jit(solution)/shard_map/ppermute | solution.py:46
  278.3 48.4 %collective-permute-start.48 = (f32[512,512]{1,0:T(8,128)}, f32[512,512]{1,0:T(8,128)}, u32[]{:S(2)}, u32[]{:S(2)}) collective-permute-start(f32[512,512]{1,0:T(8,128)} %shard_map.453), channel_id=1, source_target_pairs={{0,4},{1,5},{2,7},{3,6},{4,1},{5,0},{6,2},{7,3},{8,12},{9,13},{10,... | collective-permute-start | bytes 3145736 | tf_op jit(solution)/shard_map/ppermute | solution.py:46
  321.0 62.9 %collective-permute-start.39 = (f32[512,1024]{1,0:T(8,128)}, f32[512,1024]{1,0:T(8,128)}, u32[]{:S(2)}, u32[]{:S(2)}) collective-permute-start(f32[512,1024]{1,0:T(8,128)} %convolution_bitcast_fusion), channel_id=1, source_target_pairs={{0,2},{1,3},{2,0},{3,1},{4,6},{5,7},{6,4},{7,5},{8,10},{9,11},{10,... | collective-permute-start | bytes 6291464 | tf_op jit(solution)/shard_map/ppermute | solution.py:46
  348.5 67.5 %collective-permute-start.55 = (f32[2,256,1024]{2,1,0:T(8,128)}, f32[2,256,1024]{2,1,0:T(8,128)}, u32[]{:S(2)}, u32[]{:S(2)}) collective-permute-start(f32[2,256,1024]{2,1,0:T(8,128)} %shard_map.455), channel_id=1, source_target_pairs={{0,32},{1,33},{2,98},{3,99},{4,36},{5,37},{6,102},{7,103},{8,40},{... | collective-permute-start | bytes 6291464 | tf_op jit(solution)/shard_map/ppermute | solution.py:46
  353.7 96.0 %collective-permute-start.64 = (f32[2,256,1024]{2,1,0:T(8,128)}, f32[2,256,1024]{2,1,0:T(8,128)}, u32[]{:S(2)}, u32[]{:S(2)}) collective-permute-start(f32[2,256,1024]{2,1,0:T(8,128)} %shard_map.459), channel_id=1, source_target_pairs={{0,8},{1,9},{2,26},{3,27},{4,12},{5,13},{6,30},{7,31},{8,16},{9,17... | collective-permute-start | bytes 6291464 | tf_op jit(solution)/shard_map/ppermute | solution.py:46
  359.2 39.6 %collective-permute-start.51 = (f32[4,32,512]{2,1,0:T(8,128)}, f32[4,32,512]{2,1,0:T(8,128)S(1)}, u32[]{:S(2)}, u32[]{:S(2)}) collective-permute-start(f32[4,32,512]{2,1,0:T(8,128)} %bitcast_add_fusion.13), channel_id=1, source_target_pairs={{0,32},{1,33},{2,98},{3,99},{4,36},{5,37},{6,102},{7,103},{8,40},{... | collective-permute-start | bytes 786440 | tf_op jit(solution)/shard_map/ppermute | solution.py:46
  397.9 27.9 %collective-permute-start.100 = (f32[2,512,256]{2,1,0:T(8,128)}, f32[2,512,256]{2,1,0:T(8,128)}, u32[]{:S(2)}, u32[]{:S(2)}) collective-permute-start(f32[2,512,256]{2,1,0:T(8,128)} %shard_map.475), channel_id=1, source_target_pairs={{0,8},{1,9},{2,26},{3,27},{4,12},{5,13},{6,30},{7,31},{8,16},{9,17... | collective-permute-start | bytes 3145736 | tf_op jit(solution)/shard_map/ppermute | solution.py:46
  424.0 92.6 %collective-permute-start.56 = (f32[2,256,1024]{2,1,0:T(8,128)}, f32[2,256,1024]{2,1,0:T(8,128)}, u32[]{:S(2)}, u32[]{:S(2)}) collective-permute-start(f32[2,256,1024]{2,1,0:T(8,128)} %shard_map.456), channel_id=1, source_target_pairs={{0,32},{1,33},{2,98},{3,99},{4,36},{5,37},{6,102},{7,103},{8,40},{... | collective-permute-start | bytes 6291464 | tf_op jit(solution)/shard_map/ppermute | solution.py:46
  430.8 64.0 %collective-permute-start.101 = (f32[2,512,256]{2,1,0:T(8,128)}, f32[2,512,256]{2,1,0:T(8,128)}, u32[]{:S(2)}, u32[]{:S(2)}) collective-permute-start(f32[2,512,256]{2,1,0:T(8,128)} %shard_map.476), channel_id=1, source_target_pairs={{0,8},{1,9},{2,26},{3,27},{4,12},{5,13},{6,30},{7,31},{8,16},{9,17... | collective-permute-start | bytes 3145736 | tf_op jit(solution)/shard_map/ppermute | solution.py:46
  435.2 34.9 %collective-permute-start.93 = (f32[2,256,256]{2,1,0:T(8,128)}, f32[2,256,256]{2,1,0:T(8,128)}, u32[]{:S(2)}, u32[]{:S(2)}) collective-permute-start(f32[2,256,256]{2,1,0:T(8,128)} %shard_map.473), channel_id=1, source_target_pairs={{0,32},{1,33},{2,98},{3,99},{4,36},{5,37},{6,102},{7,103},{8,40},{... | collective-permute-start | bytes 1572872 | tf_op jit(solution)/shard_map/ppermute | solution.py:46
  448.2 61.7 %collective-permute-start.82 = (f32[512,768]{1,0:T(8,128)}, f32[512,768]{1,0:T(8,128)}, u32[]{:S(2)}, u32[]{:S(2)}) collective-permute-start(f32[512,768]{1,0:T(8,128)} %shard_map.467), channel_id=1, source_target_pairs={{0,4},{1,5},{2,7},{3,6},{4,1},{5,0},{6,2},{7,3},{8,12},{9,13},{10,... | collective-permute-start | bytes 4718600 | tf_op jit(solution)/shard_map/ppermute | solution.py:46
  468.8 61.0 %collective-permute-start.65 = (f32[2,256,1024]{2,1,0:T(8,128)S(1)}, f32[2,256,1024]{2,1,0:T(8,128)}, u32[]{:S(2)}, u32[]{:S(2)}) collective-permute-start(f32[2,256,1024]{2,1,0:T(8,128)S(1)} %shard_map.460), channel_id=1, source_target_pairs={{0,8},{1,9},{2,26},{3,27},{4,12},{5,13},{6,30},{7,31},{8,16},{9,17... | collective-permute-start | bytes 6291464 | tf_op jit(solution)/shard_map/ppermute | solution.py:46
  510.0 33.6 %collective-permute-start.45 = (f32[6,1024]{1,0:T(8,128)S(1)}, f32[6,1024]{1,0:T(8,128)S(1)}, u32[]{:S(2)}, u32[]{:S(2)}) collective-permute-start(f32[6,1024]{1,0:T(8,128)S(1)} %add.884), channel_id=1, source_target_pairs={{0,64},{1,65},{2,66},{3,67},{4,68},{5,69},{6,70},{7,71},{8,72},{9,... | collective-permute-start | bytes 73736 | tf_op jit(solution)/shard_map/ppermute | solution.py:46
  516.7 35.3 %collective-permute-start.83 = (f32[512,768]{1,0:T(8,128)}, f32[512,768]{1,0:T(8,128)}, u32[]{:S(2)}, u32[]{:S(2)}) collective-permute-start(f32[512,768]{1,0:T(8,128)} %shard_map.468), channel_id=1, source_target_pairs={{0,4},{1,5},{2,7},{3,6},{4,1},{5,0},{6,2},{7,3},{8,12},{9,13},{10,... | collective-permute-start | bytes 4718600 | tf_op jit(solution)/shard_map/ppermute | solution.py:46
  524.6 33.2 %collective-permute-start.57 = (f32[2,256,1024]{2,1,0:T(8,128)}, f32[2,256,1024]{2,1,0:T(8,128)}, u32[]{:S(2)}, u32[]{:S(2)}) collective-permute-start(f32[2,256,1024]{2,1,0:T(8,128)} %shard_map.457), channel_id=1, source_target_pairs={{0,32},{1,33},{2,98},{3,99},{4,36},{5,37},{6,102},{7,103},{8,40},{... | collective-permute-start | bytes 6291464 | tf_op jit(solution)/shard_map/ppermute | solution.py:46
  534.9 42.0 %collective-permute-start.66 = (f32[2,256,1024]{2,1,0:T(8,128)}, f32[2,256,1024]{2,1,0:T(8,128)}, u32[]{:S(2)}, u32[]{:S(2)}) collective-permute-start(f32[2,256,1024]{2,1,0:T(8,128)} %shard_map.461), channel_id=1, source_target_pairs={{0,8},{1,9},{2,26},{3,27},{4,12},{5,13},{6,30},{7,31},{8,16},{9,17... | collective-permute-start | bytes 6291464 | tf_op jit(solution)/shard_map/ppermute | solution.py:46
  555.3 27.0 %collective-permute-start.84 = (f32[512,768]{1,0:T(8,128)S(1)}, f32[512,768]{1,0:T(8,128)S(1)}, u32[]{:S(2)}, u32[]{:S(2)}) collective-permute-start(f32[512,768]{1,0:T(8,128)S(1)} %shard_map.469), channel_id=1, source_target_pairs={{0,4},{1,5},{2,7},{3,6},{4,1},{5,0},{6,2},{7,3},{8,12},{9,13},{10,... | collective-permute-start | bytes 4718600 | tf_op jit(solution)/shard_map/ppermute | solution.py:46
  (222 other events, 2389.4 us)

commit v2 on v1

v2 whole, which is shorter than its diff:
```python
import functools

import jax
import jax.numpy as jnp
import numpy as np
from jax import lax
from jax.experimental import pallas as pl
from jax.experimental.pallas import tpu as pltpu
from jax.sharding import Mesh
from jax.sharding import PartitionSpec as P

HEAD_DIM = 64
BLK = 64
CLIPS_DEV = 4
STEP = 10


LAYER_EPS = 1e-05
SAMPLE_RATE = 44100.0
LOG_TWO_NATS = 0.6931471805599453
CLIP_NORM = 1.0
BETA_FIRST = 0.9
BETA_SECOND = 0.95
ADAM_EPSILON = 1e-08
WEIGHT_DECAY = 0.01
RATE_MATRIX = 0.1
RATE_TABLE = 1.0
RATE_NORMS = 1.0
SQUARE_SCALE = 2.0**-9

AXES = ("z", "x", "yl", "c", "yh")
SIZES = (4, 4, 2, 2, 2)
DP = ("z", "x", "yl", "c")
VMEM_LIMIT = 40 * 1024 * 1024
QUERY_ROWS = 256
BF16 = jnp.bfloat16
F32 = jnp.float32


def send(value, move):
    pairs = []
    for index in range(int(np.prod(SIZES))):
        z, x, yl, c, yh = (int(i) for i in np.unravel_index(index, SIZES))
        target = move(z, x, yh * 2 + yl, c)
        if target is not None:
            z, x, y, c = target
            y %= 4
            at = (z % 4, x % 4, y % 2, c, y // 2)
            pairs.append((index, int(np.ravel_multi_index(at, SIZES))))
    return lax.ppermute(value, AXES, pairs)


def swap_core(value):
    return send(value, lambda z, x, y, c: (z, x, y, 1 - c))


def pair_sum(value):
    return value + swap_core(value)


def ring(axis):
    def move(z, x, y, c):
        step = 1 - 2 * c
        return {"z": (z + step, x, y, c), "x": (z, x + step, y, c), "y": (z, x, y + step, c)}[axis]

    return move


def by(axis, count):
    def move(z, x, y, c):
        return {"z": (z + count, x, y, c), "x": (z, x + count, y, c), "y": (z, x, y + count, c)}[axis]

    return move


def flipped(axis, bit):
    def move(z, x, y, c):
        return {"z": (z ^ bit, x, y, c), "x": (z, x ^ bit, y, c), "y": (z, x, y ^ bit, c)}[axis]

    return move


def after(value, *earlier):
    return lax.optimization_barrier((value, *earlier))[0]


def own_quarter(half, core):
    width = half.shape[-1] // 2
    return jnp.where(core == 0, half[..., :width], half[..., width:])


def row_block(native, core, block):
    slots, rows, width = native.shape
    view = native.reshape(slots, rows // 64, 64, width)
    rows_here = lax.dynamic_slice_in_dim(view, block, 1, 1)[:, 0]
    return own_quarter(rows_here, core).astype(F32)


def place_kernel(rings, s_ref, native_ref, *rest):
    out_ref = rest[-1]
    width = native_ref.shape[-1]
    part = width // len(rings)
    out_ref[0, :, :width] = native_ref[0]
    z, x, sign = s_ref[0], s_ref[1], s_ref[2]
    for r, axis in enumerate(rings):
        lanes = slice(width + r * part, width + (r + 1) * part)
        for j in range(4):
            for i in range(4):
                z_at = lax.rem(z - sign * (j if axis == "z" else i) + 8, 4)
                x_at = lax.rem(x - sign * (j if axis == "x" else i) + 8, 4)
                rows = pl.ds(pl.multiple_of(z_at * 256 + x_at * 64, 64), 64)
                out_ref[0, rows, lanes] = rest[4 * r + j][i].astype(BF16)


def place(native, first_slot, slots, rings, buffers, scalars):
    rows, width = native.shape[1], native.shape[2] // 2
    block = pl.BlockSpec((4, 64, width // len(rings)), lambda k, s: (0, 0, k))
    return pl.pallas_call(
        functools.partial(place_kernel, rings),
        grid_spec=pltpu.PrefetchScalarGridSpec(
            num_scalar_prefetch=1,
            grid=(slots,),
            in_specs=[pl.BlockSpec((1, rows, width), lambda k, s: (first_slot + k, 0, s[3]))]
            + [block] * len(buffers),
            out_specs=pl.BlockSpec((1, rows, 2 * width), lambda k, s: (k, 0, 0)),
        ),
        out_shape=jax.ShapeDtypeStruct((slots, rows, 2 * width), BF16),
        compiler_params=pltpu.CompilerParams(vmem_limit_bytes=VMEM_LIMIT),
        cost_estimate=estimate(1, 1),
    )(scalars, native, *buffers)


def place_halves_kernel(s_ref, native_ref, near_ref, far_ref, out_ref):
    half, width = near_ref.shape
    out_ref[:, :width] = native_ref[...]
    near = s_ref[4]
    out_ref[pl.ds(pl.multiple_of(near * half, 64), half), width:] = near_ref[...].astype(BF16)
    out_ref[pl.ds(pl.multiple_of((1 - near) * half, 64), half), width:] = far_ref[...].astype(BF16)


def place_halves(native, near, far, scalars):
    rows, width = native.shape[0], native.shape[1] // 2
    whole = pl.BlockSpec((rows // 2, width), lambda k, s: (0, 0))
    return pl.pallas_call(
        place_halves_kernel,
        grid_spec=pltpu.PrefetchScalarGridSpec(
            num_scalar_prefetch=1,
            grid=(1,),
            in_specs=[pl.BlockSpec((rows, width), lambda k, s: (0, s[3])), whole, whole],
            out_specs=pl.BlockSpec((rows, 2 * width), lambda k, s: (0, 0)),
        ),
        out_shape=jax.ShapeDtypeStruct((rows, 2 * width), BF16),
        compiler_params=pltpu.CompilerParams(vmem_limit_bytes=VMEM_LIMIT),
        cost_estimate=pl.CostEstimate(
            flops=0, bytes_accessed=rows * width * 10, transcendentals=0
        ),
    )(scalars, native, near, far)


def direct(value, axis):
    return jnp.stack([value] + [send(value, by(axis, k)) for k in (1, 2, 3)])


def around(buffer, axis):
    buffers = [buffer]
    for _ in range(3):
        buffers.append(send(buffers[-1], ring(axis)))
    return buffers


class Ring:
    def __init__(self, axis, place_at, sign, part):
        self.axis, self.place_at, self.sign, self.part = axis, place_at, sign, part
        self.step = 1
        self.total = part(lax.rem(place_at - sign + 8, 4))

    def arrive(self):
        return send(self.total, ring(self.axis))

    def add(self, arrived):
        self.step += 1
        own = lax.rem(self.place_at - self.step * self.sign + 8, 4)
        self.total = self.part(own, arrived)


def rows_of(grad, outer):
    view = grad.reshape(outer, 4, -1, grad.shape[1])

    def part(k, arrived=None):
        own = lax.dynamic_index_in_dim(view, k, 1, False).reshape(-1, grad.shape[1])
        return added(own, arrived)

    return part


def added(product, arrived):
    return product if arrived is None else product + arrived


def ring_x(spot, left, right):
    def part(k, arrived=None):
        rows = lax.dynamic_index_in_dim(left, k, 1, False).reshape(-1, left.shape[-1])
        return added(jnp.dot(rows, right, preferred_element_type=F32), arrived)

    return Ring("x", spot.x, spot.sign, part)


def ring_y(spot, left, right_own, right_other):
    def part(k, arrived=None):
        rows = lax.dynamic_index_in_dim(left, lax.rem(k, 2), 1, False).reshape(-1, left.shape[-1])
        right = jnp.where(lax.div(k, 2) == spot.yh, right_own, right_other)
        return added(jnp.dot(rows, right, preferred_element_type=F32), arrived)

    return Ring("y", spot.y, spot.sign, part)


def scatter_z(grad):
    return lax.psum_scatter(grad, "z", scatter_dimension=0, tiled=True)


def direct_y(spot, grad, rows):
    width = grad.shape[1] // 2
    view = grad.reshape(-1, 2, rows, 2 * width)
    same = lax.dynamic_index_in_dim(view, spot.yl, 1, False)
    other = lax.dynamic_index_in_dim(view, 1 - spot.yl, 1, False)
    near = send(other[..., :width], flipped("y", 1))
    far = send(other[..., width:], flipped("y", 3))
    across = send(same[..., width:], flipped("y", 2))
    return ((same[..., :width] + near) + (far + across)).reshape(-1, width)


def direct_sum(axis, place_at, grad, outer=1):
    view = grad.reshape(outer, 4, grad.shape[0] // (4 * outer), grad.shape[1])
    parts = [
        send(lax.dynamic_index_in_dim(view, lax.rem(place_at + k, 4), 1, False), by(axis, k))
        for k in (1, 2, 3)
    ]
    own = lax.dynamic_index_in_dim(view, place_at, 1, False)
    return ((own + parts[0]) + (parts[1] + parts[2])).reshape(-1, grad.shape[1])


def turned(value):
    return lax.optimization_barrier(value.T)


class Spot:
    def __init__(self):
        self.z, self.x, self.yl, self.c, self.yh = (lax.axis_index(a) for a in AXES)
        self.y = self.yh * 2 + self.yl
        self.sign = 1 - 2 * self.c


def sum_of_four(value, axis, place_at):
    pieces = [value] + [send(value, by(axis, k)) for k in (1, 2, 3)]
    total = None
    for at in range(4):
        back = lax.rem(place_at - at + 4, 4)
        part = pieces[3]
        for k in (2, 1, 0):
            part = jnp.where(back == k, pieces[k], part)
        total = part if total is None else total + part
    return total


def contract(left_side, right_side, left_dim, right_dim):
    return lax.dot_general(
        left_side,
        right_side,
        (((left_dim,), (right_dim,)), ((), ())),
        preferred_element_type=jnp.float32,
    )


def attention_forward_kernel(heads_ref, mask_ref, out_ref, total_ref):
    length = heads_ref.shape[1]
    for half in range(2):
        lanes = slice(half * HEAD_DIM, (half + 1) * HEAD_DIM)
        keys, values = heads_ref[1, :, lanes], heads_ref[2, :, lanes]
        scaled = heads_ref[0, :, lanes] * jnp.asarray(HEAD_DIM ** (-0.5), BF16)
        for start in range(0, length, QUERY_ROWS):
            stop = start + QUERY_ROWS
            scores = contract(scaled[start:stop], keys[:stop], 1, 1)
            scores = jnp.where(mask_ref[start:stop, :stop] > 0, scores, -1e30)
            top = jnp.max(scores, axis=-1, keepdims=True)
            weights = jnp.exp(scores - top)
            sums = jnp.sum(weights, axis=-1, keepdims=True)
            weights = (weights * (1.0 / sums)).astype(BF16)
            out_ref[start:stop, lanes] = contract(weights, values[:stop], 1, 0).astype(BF16)
            total_ref[0, start:stop, half : half + 1] = top + jnp.log(sums)


def attention_backward_kernel(heads_ref, mask_ref, total_ref, grad_ref, out_ref, keys_acc, values_acc):
    length = heads_ref.shape[1]
    for half in range(2):
        lanes = slice(half * HEAD_DIM, (half + 1) * HEAD_DIM)
        keys, values = heads_ref[1, :, lanes], heads_ref[2, :, lanes]
        scaled = heads_ref[0, :, lanes] * jnp.asarray(HEAD_DIM ** (-0.5), BF16)
        for start in range(length - QUERY_ROWS, -1, -QUERY_ROWS):
            stop = start + QUERY_ROWS
            queries, grad = scaled[start:stop], grad_ref[start:stop, lanes]
            scores = contract(queries, keys[:stop], 1, 1)
            scores = jnp.where(mask_ref[start:stop, :stop] > 0, scores, -1e30)
            weights = jnp.exp(scores - total_ref[0, start:stop, half : half + 1])
            grad_values = contract(weights.astype(BF16), grad, 0, 0)
            grad_weights = contract(grad, values[:stop], 1, 1)
            total = jnp.sum(weights * grad_weights, axis=-1, keepdims=True)
            grad_scores = (weights * (grad_weights - total)).astype(BF16)
            grad_queries = contract(grad_scores, keys[:stop], 1, 0) * HEAD_DIM ** (-0.5)
            out_ref[0, start:stop, lanes] = grad_queries.astype(BF16)
            grad_keys = contract(grad_scores, queries, 0, 0)
            if stop == length:
                keys_acc[...] = grad_keys
                values_acc[...] = grad_values
            else:
                keys_acc[:stop] += grad_keys
                values_acc[:stop] += grad_values
        out_ref[1, :, lanes] = keys_acc[...].astype(BF16)
        out_ref[2, :, lanes] = values_acc[...].astype(BF16)


def estimate(flops, moved):
    return pl.CostEstimate(flops=flops, bytes_accessed=moved, transcendentals=0)


def attention_forward(heads, mask):
    length, width = heads.shape[1:]
    return pl.pallas_call(
        attention_forward_kernel,
        grid=(width // 128,),
        in_specs=[
            pl.BlockSpec((3, length, 128), lambda g: (0, 0, g)),
            pl.BlockSpec((length, length), lambda g: (0, 0)),
        ],
        out_specs=[
            pl.BlockSpec((length, 128), lambda g: (0, g)),
            pl.BlockSpec((1, length, 2), lambda g: (g, 0, 0)),
        ],
        out_shape=[
            jax.ShapeDtypeStruct((length, width), BF16),
            jax.ShapeDtypeStruct((width // 128, length, 2), F32),
        ],
        compiler_params=pltpu.CompilerParams(vmem_limit_bytes=VMEM_LIMIT),
        cost_estimate=estimate(1, 1),
    )(heads, mask)


def attention_backward(heads, mask, totals, grad_mixed):
    length, width = heads.shape[1:]
    return pl.pallas_call(
        attention_backward_kernel,
        grid=(width // 128,),
        in_specs=[
            pl.BlockSpec((3, length, 128), lambda g: (0, 0, g)),
            pl.BlockSpec((length, length), lambda g: (0, 0)),
            pl.BlockSpec((1, length, 2), lambda g: (g, 0, 0)),
            pl.BlockSpec((length, 128), lambda g: (0, g)),
        ],
        out_specs=pl.BlockSpec((3, length, 128), lambda g: (0, 0, g)),
        out_shape=jax.ShapeDtypeStruct((3, length, width), BF16),
        scratch_shapes=[pltpu.VMEM((length, HEAD_DIM), F32), pltpu.VMEM((length, HEAD_DIM), F32)],
        compiler_params=pltpu.CompilerParams(vmem_limit_bytes=VMEM_LIMIT),
        cost_estimate=estimate(1, 1),
    )(heads, mask, totals, grad_mixed)


def feedforward_backward_kernel(block_ref, down_ref, pre_ref, up_ref, grad_pre_ref, normed_ref):
    grad_activated = jnp.dot(block_ref[...], down_ref[...], preferred_element_type=F32)
    pre = pre_ref[...]
    slope = 0.7978845608028654
    bent = jnp.tanh(slope * (pre + 0.044715 * pre * pre * pre))
    inner = slope * (1.0 + 3.0 * 0.044715 * pre * pre)
    factor = 0.5 * (1.0 + bent) + 0.5 * pre * (1.0 - bent * bent) * inner
    grad_pre = (grad_activated * factor).astype(BF16)
    grad_pre_ref[...] = grad_pre
    part = contract(grad_pre, up_ref[...], 1, 1)

    @pl.when(pl.program_id(0) == 0)
    def _():
        normed_ref[...] = part

    @pl.when(pl.program_id(0) > 0)
    def _():
        normed_ref[...] += part


def feedforward_backward(block_low, down_full, pre_act, up_full):
    length, hidden = pre_act.shape
    width, tile = block_low.shape[1], 512
    return pl.pallas_call(
        feedforward_backward_kernel,
        grid=(hidden // tile,),
        in_specs=[
            pl.BlockSpec((length, width), lambda g: (0, 0)),
            pl.BlockSpec((width, tile), lambda g: (0, g)),
            pl.BlockSpec((length, tile), lambda g: (0, g)),
            pl.BlockSpec((width, tile), lambda g: (0, g)),
        ],
        out_specs=[
            pl.BlockSpec((length, tile), lambda g: (0, g)),
            pl.BlockSpec((length, width), lambda g: (0, 0)),
        ],
        out_shape=[
            jax.ShapeDtypeStruct((length, hidden), BF16),
            jax.ShapeDtypeStruct((length, width), F32),
        ],
        compiler_params=pltpu.CompilerParams(vmem_limit_bytes=VMEM_LIMIT),
        cost_estimate=estimate(1, 1),
    )(block_low, down_full, pre_act, up_full)


def norm_rows(values, gain_row, shift_row):
    average = jnp.mean(values, axis=-1, keepdims=True)
    centred = values - average
    variance = jnp.mean(centred * centred, axis=-1, keepdims=True)
    return centred * lax.rsqrt(variance + LAYER_EPS) * gain_row + shift_row


def allowed_mask(segments, layout):
    length = segments.shape[0]
    position = jnp.arange(length)
    blocks = layout.shape[0]
    block_open = (
        jnp.broadcast_to(layout[:, None, :, None], (blocks, BLK, blocks, BLK)).reshape(
            length, length
        )
        > 0
    )
    causal = position[None, :] <= position[:, None]
    return causal & (segments[:, None] == segments[None, :]) & block_open


def layer_forward(residual, project_weight, mix_weight, up_weight, down_weight, norm_gains, mask, early):
    normed_one = norm_rows(residual, norm_gains[0], norm_gains[1]).astype(jnp.bfloat16)
    heads = jnp.einsum(
        "td,sde->ste", normed_one, project_weight, preferred_element_type=jnp.float32
    ).astype(jnp.bfloat16)
    heads = after(heads, *early[0])
    mixed_low, totals = attention_forward(heads, mask)
    mixed_low = after(mixed_low, *early[1])
    after_attention = residual + pair_sum(contract(mixed_low, mix_weight, 1, 1))
    normed_two = norm_rows(after_attention, norm_gains[2], norm_gains[3]).astype(jnp.bfloat16)
    normed_two = after(normed_two, *early[2])
    pre_act = jnp.dot(normed_two, up_weight, preferred_element_type=jnp.float32)
    activated = jax.nn.gelu(pre_act).astype(jnp.bfloat16)
    activated = after(activated, *early[3])
    after_block = after_attention + pair_sum(contract(activated, down_weight, 1, 1))
    saved_state = (
        residual,
        normed_one,
        heads,
        totals,
        mixed_low,
        after_attention,
        normed_two,
        pre_act,
        activated,
    )
    return (after_block, saved_state)


def head_loss(after_block, output_table, norm_gains, code_tokens, segments, keep_flag, spot):
    normed_three = norm_rows(after_block, norm_gains[4], norm_gains[5]).astype(jnp.bfloat16)
    logits = jnp.dot(normed_three, output_table, preferred_element_type=jnp.float32)
    width = output_table.shape[1]
    quarter = width // 2
    targets = jnp.concatenate([code_tokens[1:], code_tokens[-1:]])
    column = jnp.arange(width)
    code = jnp.where(
        column < quarter,
        spot.yh * width + spot.c * quarter + column,
        (1 - spot.yh) * width + spot.c * quarter + column - quarter,
    )
    target_hit = code[None, :] == targets[:, None]
    row_top = jnp.max(logits, axis=1)
    row_sums = jnp.sum(jnp.exp(logits - row_top[:, None]), axis=1)
    picked = jnp.sum(jnp.where(target_hit, logits, 0.0), axis=1)
    other = swap_core(jnp.stack([row_top, row_sums, picked]))
    both_top = jnp.maximum(row_top, other[0])
    both_sums = row_sums * jnp.exp(row_top - both_top) + other[1] * jnp.exp(other[0] - both_top)
    log_norm = both_top + jnp.log(both_sums)
    next_segment = jnp.concatenate([segments[1:], jnp.full((1,), -1, jnp.int32)])
    counted = ((segments == next_segment) & (segments < CLIPS_DEV)).astype(jnp.float32) * keep_flag
    loss_local = jnp.sum(counted * (log_norm - (picked + other[2]))) / LOG_TWO_NATS
    grad_logits = (counted / LOG_TWO_NATS)[:, None] * (
        jnp.exp(logits - log_norm[:, None]) - target_hit.astype(jnp.float32)
    )
    grad_low = grad_logits.astype(jnp.bfloat16)
    return (loss_local, normed_three, grad_low)


def norm_backward(values, gain_row, shift_row, grad_normed):
    _, pullback = jax.vjp(norm_rows, values, gain_row, shift_row)
    return pullback(grad_normed)


def adam_step(gradient, master, first_old, second_old, step_rate, decay_rate):
    moment = BETA_FIRST * first_old + (1.0 - BETA_FIRST) * gradient
    variance = BETA_SECOND * second_old + (1.0 - BETA_SECOND) * gradient * gradient
    moment_hat = moment / (1.0 - BETA_FIRST**STEP)
    variance_hat = variance / (1.0 - BETA_SECOND**STEP)
    updated = master - step_rate * (
        moment_hat / (jnp.sqrt(variance_hat) + ADAM_EPSILON) + decay_rate * master
    )
    return (moment, variance, updated)


def local(
    code_tokens,
    segments,
    layout,
    durations,
    overflow,
    upper_context,
    embed_table,
    condition_weight,
    attention_weight,
    feedforward_weight,
    output_table,
    norm_gains,
    embed_master,
    condition_master,
    attention_master,
    feedforward_master,
    output_master,
    norms_master,
    embed_first,
    condition_first,
    attention_first,
    feedforward_first,
    output_first,
    norms_first,
    embed_second,
    condition_second,
    attention_second,
    feedforward_second,
    output_second,
    norms_second,
):
    spot = Spot()
    core, yh = spot.c, spot.yh
    settled = core == yh
    length = code_tokens.shape[0]

    keep_native = 1.0 - overflow[0].astype(jnp.float32)
    local_seconds = keep_native * jnp.sum(durations.astype(jnp.float32)) / SAMPLE_RATE
    native_ints = jnp.concatenate([code_tokens, segments, jnp.broadcast_to(overflow, (128,))])
    window_ints = jnp.where(settled, native_ints, swap_core(native_ints))
    window_tokens = window_ints[:length]
    window_segments = window_ints[length : 2 * length]
    keep_flag = 1.0 - window_ints[2 * length].astype(jnp.float32)

    def crossed(value):
        return send(value, lambda z, x, y, c: (z, x, 3 - y, c))

    block = spot.z * 4 + spot.x
    barrier = lax.optimization_barrier
    project_rows = row_block(attention_weight, core, block)[:3]
    feedforward_rows = row_block(feedforward_weight, core, block)
    pieces = crossed(
        jnp.concatenate([*project_rows, feedforward_rows[1], feedforward_rows[0]], axis=1)
    )
    quarter = project_rows.shape[2]

    embedded = jnp.take(embed_table, code_tokens, axis=0).astype(F32)
    half_width = embed_table.shape[1]
    embed_part = contract(upper_context, condition_weight, 1, 1)
    embed_part = jnp.concatenate(
        [
            embed_part[:, :half_width] + jnp.where(yh == 0, embedded, 0.0),
            embed_part[:, half_width:] + jnp.where(yh == 1, embedded, 0.0),
        ],
        axis=1,
    )
    embed_part, pieces = barrier((embed_part, pieces))
    from_other = send(
        embed_part,
        lambda z, x, y, c: (z, x, y ^ 2, c) if c != y // 2 else None,
    )
    first, second = [pieces[:, : 5 * quarter]], [pieces[:, 5 * quarter :]]
    for _ in range(3):
        arrived = barrier((send(first[-1], ring("x")), send(second[-1], ring("z"))))
        first.append(arrived[0])
        second.append(arrived[1])
    first, second = jnp.stack(first), jnp.stack(second)
    first, second, from_other = barrier((first, second, from_other))
    window_sum = embed_part + from_other
    residual = jnp.where(settled, window_sum, swap_core(window_sum))

    def half_rows(native):
        halves = own_quarter(native, core).reshape(2, native.shape[0] // 2, -1)
        return lax.dynamic_index_in_dim(halves, 1 - spot.yl, 0, False).astype(F32)

    mix_half, output_half, residual = barrier(
        (half_rows(attention_weight[3]), half_rows(output_table), residual)
    )
    project_buffers = [first[:, :, : 3 * quarter]]
    up_buffers = [second[:, :, 2 * quarter :]]
    on_y = [mix_half]
    for move in (lambda z, x, y, c: (z, x, 3 - y, c), flipped("y", 1), lambda z, x, y, c: (z, x, 3 - y, c)):
        value = output_half if len(on_y) == 3 else on_y[-1]
        arrived = barrier(
            (send(project_buffers[-1], ring("z")), send(up_buffers[-1], ring("x")), send(value, move))
        )
        for buffers, value in zip((project_buffers, up_buffers, on_y), arrived, strict=True):
            buffers.append(value)
    mix_near, mix_far, output_near = on_y[1:]
    down_low, down_high = [first[:, :, 3 * quarter :]], [second[:, :, : 2 * quarter]]
    down_low[0], down_high[0], *_ = barrier((down_low[0], down_high[0], output_near))
    for k in range(3):
        arrived = [send(down_low[-1], ring("z")), send(down_high[-1], ring("x"))]
        if k == 0:
            arrived.append(send(output_near, flipped("y", 1)))
        arrived = barrier(tuple(arrived))
        down_low.append(arrived[0])
        down_high.append(arrived[1])
        if k == 0:
            output_far = arrived[2]

    scalars = jnp.stack([spot.z, spot.x, spot.sign, core, spot.yl]).astype(jnp.int32)
    project_full = place(attention_weight, 0, 3, ("z",), project_buffers, scalars)
    mix_full = place_halves(attention_weight[3], mix_near, mix_far, scalars)
    up_full = place(feedforward_weight, 0, 1, ("x",), up_buffers, scalars)[0]
    down_full = place(feedforward_weight, 1, 1, ("z", "x"), down_low + down_high, scalars)[0]
    output_full = place_halves(output_table, output_near, output_far, scalars)

    width = half_width // 2
    context_own = own_quarter(upper_context, core).astype(F32)
    context_sibling = own_quarter(upper_context, 1 - core).astype(F32)
    context_arrived = swap_core(context_sibling)
    context_near = jnp.where(settled, context_own, context_arrived)
    context_far = send(
        after(jnp.where(settled, context_arrived, context_own), output_far), by("y", 2)
    )

    allowed = allowed_mask(window_segments, layout).astype(F32)
    after_block, saved_state = layer_forward(
        residual,
        project_full,
        mix_full,
        up_full,
        down_full,
        norm_gains,
        allowed,
        (
            (mix_full, up_full, down_low[1]),
            (down_low[2], output_far),
            (down_low[3],),
            (context_far,),
        ),
    )
    residual, normed_one, heads, totals, mixed_low = saved_state[:5]
    after_attention, normed_two, pre_act, activated = saved_state[5:]
    loss_local, normed_three, grad_logits = head_loss(
        after_block, output_full, norm_gains, window_tokens, window_segments, keep_flag, spot
    )
    left_three = turned(normed_three).reshape(16, 2, 32, length)
    left_two = turned(normed_two).reshape(4, 4, 64, length)
    left_one = turned(normed_one).reshape(16, 2, 32, length)

    grad_normed = pair_sum(contract(grad_logits, output_full, 1, 1))
    output_ring = ring_y(spot, left_three, grad_logits[:, :512], grad_logits[:, 512:])
    grad_normed = after(grad_normed, output_ring.total)
    grad_block, *norm_three = norm_backward(after_block, norm_gains[4], norm_gains[5], grad_normed)
    block_low = grad_block.astype(BF16)
    down_grad = contract(block_low, activated, 0, 0)
    down_z = scatter_z(down_grad)
    block_low = after(block_low, down_grad)

    grad_pre, normed_part = feedforward_backward(block_low, down_full, pre_act, up_full)
    output_one = output_ring.arrive()
    normed_part = after(normed_part, output_one)
    grad_normed = pair_sum(normed_part)
    up_ring = ring_x(spot, left_two, grad_pre)
    output_ring.add(output_one)
    grad_normed = after(grad_normed, up_ring.total, output_ring.total)
    grad_input, *norm_two = norm_backward(
        after_attention, norm_gains[2], norm_gains[3], grad_normed
    )
    grad_attention = grad_block + grad_input
    attention_low = grad_attention.astype(BF16)
    grad_mixed = jnp.dot(attention_low, mix_full, preferred_element_type=F32).astype(BF16)
    grad_projected = attention_backward(heads, allowed, totals, grad_mixed)
    grad_projected, up_one, output_two = barrier(
        (grad_projected, up_ring.arrive(), output_ring.arrive())
    )
    up_ring.add(up_one)
    output_ring.add(output_two)
    grad_projected = after(grad_projected, up_ring.total, output_ring.total)
    quarter = grad_projected.shape[2] // 2
    project_ring = ring_y(
        spot,
        left_one,
        jnp.concatenate([grad_projected[k, :, :quarter] for k in range(3)], axis=1),
        jnp.concatenate([grad_projected[k, :, quarter:] for k in range(3)], axis=1),
    )
    normed_part = jnp.einsum(
        "ste,sde->td", grad_projected, project_full, preferred_element_type=F32
    )
    grad_normed = pair_sum(after(normed_part, project_ring.total))
    grad_input, *norm_one = norm_backward(residual, norm_gains[0], norm_gains[1], grad_normed)
    grad_residual = grad_attention + grad_input

    context_far = context_far + 0.0 * local_seconds
    context = jnp.concatenate([context_near, context_far], axis=1).astype(BF16)

    def columns_of(half):
        side = jnp.where(half == 0, grad_residual[:, : 2 * width], grad_residual[:, 2 * width :])
        return own_quarter(side, core)

    own_grad = jnp.concatenate([columns_of(yh), columns_of(1 - yh)], axis=1)
    own_high = own_grad.astype(BF16)
    own_low = (own_grad - own_high.astype(F32)).astype(BF16)
    hot = (jnp.arange(embed_table.shape[0])[:, None] == window_tokens[None, :]).astype(BF16)
    embed_grad = jnp.dot(hot, own_high, preferred_element_type=F32) + jnp.dot(
        hot, own_low, preferred_element_type=F32
    )
    embed_z = scatter_z(embed_grad)
    small_left = barrier(
        (attention_low.T.reshape(4, 4, 64, length), grad_residual.astype(BF16).T.reshape(4, 4, 64, length))
    )

    def small_part(k, arrived=None):
        parts = [
            jnp.dot(
                lax.dynamic_index_in_dim(left, k, 1, False).reshape(-1, length),
                right,
                preferred_element_type=F32,
            )
            for left, right in zip(small_left, (mixed_low, context), strict=True)
        ]
        return added(jnp.concatenate(parts, axis=1), arrived)

    small_ring = Ring("x", spot.x, spot.sign, small_part)
    norms_grad = jnp.stack([*norm_one, *norm_two, *norm_three])

    up_two, output_three, project_one, first_small = barrier(
        (up_ring.arrive(), output_ring.arrive(), project_ring.arrive(), small_ring.total)
    )
    up_ring.add(up_two)
    project_ring.add(project_one)
    output_ring.add(output_three)
    small_ring.total = first_small
    output_y = output_ring.total
    up_three, project_two, small_one, down_z = barrier(
        (up_ring.arrive(), project_ring.arrive(), small_ring.arrive(), down_z)
    )
    up_ring.add(up_three)
    project_ring.add(project_two)
    small_ring.add(small_one)
    up_x = up_ring.total
    down_ring = Ring("x", spot.x, spot.sign, rows_of(down_z, 1))
    out_ring = Ring("z", spot.z, spot.sign, rows_of(output_y, 1))
    up_zring = Ring("z", spot.z, spot.sign, rows_of(up_x, 1))
    norms = norms_grad
    norms_at = [("x", 1), ("x", 2), ("y", 1), ("y", 2), ("z", 1), ("z", 2)]

    def one_round(rings):
        nonlocal norms
        axis, bit = norms_at.pop(0)
        arrived = barrier((*[r.arrive() for r in rings], send(norms, flipped(axis, bit))))
        for r, value in zip(rings, arrived, strict=False):
            r.add(value)
        norms = norms + arrived[-1]

    one_round([project_ring, small_ring, down_ring, up_zring])
    project_zring = Ring("z", spot.z, spot.sign, rows_of(project_ring.total, 1))
    one_round([small_ring, down_ring, up_zring, project_zring])
    small_zring = Ring("z", spot.z, spot.sign, rows_of(small_ring.total, 1))
    embed_ring = Ring("x", spot.x, spot.sign, rows_of(embed_z, 1))
    one_round([down_ring, up_zring, project_zring, embed_ring])
    one_round([project_zring, small_zring, embed_ring, out_ring])
    one_round([small_zring, embed_ring, out_ring])
    one_round([small_zring, out_ring])
    norms_grad = norms
    up_z, small_z = up_zring.total, small_zring.total
    last = direct_y(
        spot,
        jnp.concatenate(
            [
                up_z[:, :1024],
                down_ring.total[:, :1024],
                small_z[:, :256],
                small_z[:, 512:768],
                up_z[:, 1024:],
                down_ring.total[:, 1024:],
                small_z[:, 256:512],
                small_z[:, 768:],
            ],
            axis=1,
        ),
        32,
    )
    embed_sum = direct_y(spot, embed_ring.total, 64)
    last_y = direct_sum(
        "x", spot.x, jnp.concatenate([out_ring.total, project_zring.total], axis=1)
    )
    output_sum, project_sum = last_y[:, :512], last_y[:, 512:]
    up_sum, down_sum = last[:, :1024], last[:, 1024:2048]
    mix_sum, condition_sum = last[:, 2048:2304], last[:, 2304:]
    dp_rank = ((spot.z * 4 + spot.x) * 2 + spot.yl) * 2 + core
    norms_share = lax.dynamic_slice_in_dim(norms_grad, dp_rank * 16, 16, 1)

    sums = [output_sum, down_sum, up_sum, mix_sum, project_sum, condition_sum, embed_sum]
    squares = 0.5 * jnp.sum((norms_share * SQUARE_SCALE) ** 2)
    for piece in sums:
        squares = squares + jnp.sum((piece * SQUARE_SCALE) ** 2)
    scalars = jnp.stack([0.5 * loss_local, squares, 0.5 * local_seconds])
    scalars = pair_sum(jnp.broadcast_to(scalars[:, None], (3, 128)))
    for axis, at in (("x", spot.x), ("z", spot.z), ("y", spot.y)):
        scalars = sum_of_four(scalars, axis, at)
    loss_total, seconds_total = scalars[0, 0], scalars[2, 0]
    inverse = 1.0 / seconds_total
    gradient_norm = jnp.sqrt(scalars[1, 0]) * (inverse / SQUARE_SCALE)
    clip_factor = CLIP_NORM / jnp.maximum(gradient_norm, CLIP_NORM)

    flat = [piece.reshape(2, 16, -1) for piece in sums[:-1]] + [sums[-1].reshape(2, 16, 512)]
    flat = jnp.concatenate(flat, axis=2)
    mine = lax.dynamic_index_in_dim(flat, core, 0, False)
    theirs = swap_core(lax.dynamic_index_in_dim(flat, 1 - core, 0, False))
    low_side = jnp.where(core == 0, mine, theirs)
    high_side = jnp.where(core == 0, theirs, mine)

    def share(start, stop):
        return low_side[:, start:stop], high_side[:, start:stop]

    output_share = jnp.concatenate(share(0, 512), axis=1)
    feedforward_share = jnp.stack(
        [jnp.concatenate(share(1536, 2560), axis=1), jnp.concatenate(share(512, 1536), axis=1)]
    )
    mix_low, mix_high = share(2560, 2816)
    project_low, project_high = share(2816, 3584)
    attention_share = jnp.stack(
        [
            jnp.concatenate(
                [project_low[:, 256 * k : 256 * k + 256], project_high[:, 256 * k : 256 * k + 256]],
                axis=1,
            )
            for k in range(3)
        ]
        + [jnp.concatenate([mix_low, mix_high], axis=1)]
    )
    condition_share = jnp.concatenate(share(3584, 3840), axis=1)
    embed_share = jnp.concatenate([part.reshape(32, 256) for part in share(3840, 4352)], axis=1)

    shares = (
        embed_share,
        condition_share,
        attention_share,
        feedforward_share,
        output_share,
        norms_share,
    )
    masters = (
        embed_master,
        condition_master,
        attention_master,
        feedforward_master,
        output_master,
        norms_master,
    )
    firsts = (
        embed_first,
        condition_first,
        attention_first,
        feedforward_first,
        output_first,
        norms_first,
    )
    seconds_old = (
        embed_second,
        condition_second,
        attention_second,
        feedforward_second,
        output_second,
        norms_second,
    )
    rates = (RATE_TABLE, RATE_MATRIX, RATE_MATRIX, RATE_MATRIX, RATE_MATRIX, RATE_NORMS)
    decays = (WEIGHT_DECAY, WEIGHT_DECAY, WEIGHT_DECAY, WEIGHT_DECAY, WEIGHT_DECAY, 0.0)
    outputs = [loss_total, seconds_total, gradient_norm]
    for slot in range(6):
        outputs += adam_step(
            shares[slot] * inverse * clip_factor,
            masters[slot],
            firsts[slot],
            seconds_old[slot],
            rates[slot],
            decays[slot],
        )
    return tuple(outputs)


def solution(mesh):
    torus = Mesh(mesh.devices.reshape(SIZES), AXES)
    table, slotted = P(DP, "yh"), P(None, DP, "yh")
    state = (table, table, slotted, slotted, table, P(None, DP))
    results = tuple(spec for spec in state for _ in range(3))
    return jax.shard_map(
        local,
        mesh=torus,
        in_specs=(
            P(DP),
            P(DP),
            P(),
            P(DP),
            P(DP),
            table,
            P(None, "yh"),
            P(None, "yh"),
            P(None, None, "yh"),
            P(None, None, "yh"),
            P(None, "yh"),
            P(),
        )
        + state * 3,
        out_specs=(P(), P(), P()) + results,
        check_vma=False,
    )
```

time: 697 us -> 589 us (0.85)
  Pallas kernels: 102 us -> 40.8 us
  waiting for transfers between devices: 187 us -> 137 us
  starting transfers between devices: 178 us -> 146 us
  between operations: 13.8 us -> 26.9 us
  matrix products: 46.5 us -> 57 us
  local copies, waits for them, and re-layouts: 67.7 us -> 77.6 us
    pallas_call x33 -> x6, Pallas kernels: 99.7 us -> 37.9 us  [the longest x1 10.8 us: feedforward_backward(): pl.pallas_call(feedforward_backward_kernel, grid=(hidden // tile,), in_sp...]
    ppermute x120 -> x90, waiting for transfers between devices: 187 us -> 137 us  [send(): return lax.ppermute(value, AXES, pairs)]
    ppermute x120 -> x90, starting transfers between devices: 178 us -> 146 us  [send(): return lax.ppermute(value, AXES, pairs)]
    dynamic_slice x0 -> x4, local copies, waits for them, and re-layouts: none -> 8.94 us  [the longest x2 3.96 us: part(): lax.dynamic_index_in_dim(left, lax.rem(k, 2), 1, False)]
    add x43 -> x34, other arithmetic: 19.5 us -> 27.1 us  [the longest x27 23.5 us: added(): return product if arrived is None else product + arrived]
    dot_general x9 -> x24, matrix products: 25.3 us -> 32.1 us  [the longest x12 19.7 us: part(): return added(jnp.dot(rows, right, preferred_element_type=F32), arrived)]
    unnamed x258 -> x279, local copies, waits for them, and re-layouts: 29.7 us -> 31.9 us
  transfers between devices with their start and end apart: 120 -> 92, of which waited for: 44 -> 40; matrix products, arithmetic and copies ran while one was open for 21% -> 26% of each run, Pallas kernels for 15% -> 7%
where the time goes in v2:
time: 589 us; the launch traced here: 578 us
  starting transfers between devices  146 us (25%)
  waiting for transfers between devices  137 us (23%)
  other arithmetic  92.4 us (16%)
  local copies, waits for them, and re-layouts  77.6 us (13%)
  matrix products  57 us (10%)
  Pallas kernels  40.8 us (7%)
  between operations  26.9 us (5%)
    ppermute x90, starting transfers between devices, send(): return lax.ppermute(value, AXES, pairs)  146 us
    ppermute x90, waiting for transfers between devices, send(): return lax.ppermute(value, AXES, pairs)  137 us
    unnamed x279, local copies, waits for them, and re-layouts  31.9 us
    add x27, other arithmetic, added(): return product if arrived is None else product + arrived  23.5 us
    dot_general x12, matrix products, part(): return added(jnp.dot(rows, right, preferred_element_type=F32), arrived)  19.7 us
    dot_general x5, matrix products, contract(): lax.dot_general(left_side, right_side, (((left_dim,), (right_dim,)), ((),...  16.3 us
  transfers between devices with their start and end apart: 92, of which 40 were waited for; matrix products, arithmetic and copies ran while one was open for 26% of the time, Pallas kernels for 7%

profile of v2, /device:TPU:1, one launch (start us, length us, event | category | flops | bytes accessed | tf_op | source)
XLA Modules:
  0.0 578.1 jit_solution(2679839257019180320)
XLA Ops:
  22.7 9.8 %collective-permute-done.1 = f32[64,2816]{1,0:T(8,128)S(1)} collective-permute-done((f32[64,2816]{1,0:T(8,128)}, f32[64,2816]{1,0:T(8,128)S(1)}, u32[]{:S(2)}, u32[]{:S(2)}) %collective-permute-start.1) | collective-permute-done | bytes 720928 | tf_op jit(solution)/shard_map/ppermute | solution.py:50
  42.5 4.0 collective-permute-done.2
  50.1 4.0 collective-permute-done.4
  58.2 4.0 collective-permute-done.6
  88.2 8.4 %collective-permute-done.12.near_ref = f32[512,256]{1,0:T(8,128)S(1)} collective-permute-done((f32[512,256]{1,0:T(8,128)S(1)}, f32[512,256]{1,0:T(8,128)S(1)}, u32[]{:S(2)}, u32[]{:S(2)}) %collective-permute-start.12) | collective-permute-done | bytes 524320 | tf_op jit(solution)/shard_map/ppermute | solution.py:50
  101.3 8.2 %collective-permute-done.15.far_ref = f32[512,256]{1,0:T(8,128)S(1)} collective-permute-done((f32[512,256]{1,0:T(8,128)S(1)}, f32[512,256]{1,0:T(8,128)S(1)}, u32[]{:S(2)}, u32[]{:S(2)}) %collective-permute-start.15) | collective-permute-done | bytes 524320 | tf_op jit(solution)/shard_map/ppermute | solution.py:50
  154.6 7.9 %shard_map.448 = (bf16[512,512]{1,0:T(8,128)(2,1)S(1)}, f32[4,512,2]{2,1,0:T(8,128)S(1)}) custom-call(bf16[3,512,512]{2,1,0:T(8,128)(2,1)S(1)} %fusion.17.heads_ref, f32[512,512]{1,0:T(8,128)S(1)} %fusion.23.mask_ref), custom_call_target="tpu_custom_call" | custom-call | flops 1 | bytes 1 | tf_op jit(solution)/shard_map/pallas_call | solution.py:327
  182.2 5.5 fusion.114
  190.6 5.1 fusion.7
  230.6 5.8 %fusion.137 = f32[1024,2048]{1,0:T(8,128)} fusion(bf16[512,1024]{1,0:T(8,128)(2,1)S(1)} %add_convert_fusion.3.block_ref, bf16[512,2048]{1,0:T(8,128)(2,1)S(1)} %copy-done.130), kind=kOutput, calls=%fused_computation.355 | convolution fusion | flops 2147483648 | bytes 11534336 | tf_op jit(solution)/shard_map/dot_general | solution.py:266
  247.5 10.8 %shard_map.451 = (bf16[512,2048]{1,0:T(8,128)(2,1)S(1)}, f32[512,1024]{1,0:T(8,128)}) custom-call(bf16[512,1024]{1,0:T(8,128)(2,1)S(1)} %copy-done.17, bf16[1024,2048]{1,0:T(8,128)(2,1)S(1)} %bitcast.294, f32[512,2048]{1,0:T(8,128)S(1)} %copy-done.15, bf16[1024,2048]{1,0:T(8,128)(2,1)} %bitcast.293), custom_call_target="tpu_custom_call" | custom-call | flops 1 | bytes 1 | tf_op jit(solution)/shard_map/pallas_call | solution.py:389
  280.3 10.0 %shard_map.452 = bf16[3,512,512]{2,1,0:T(8,128)(2,1)S(1)} custom-call(bf16[3,512,512]{2,1,0:T(8,128)(2,1)S(1)} %copy-done.14, f32[512,512]{1,0:T(8,128)S(1)} %copy-done.9, f32[4,512,2]{2,1,0:T(8,128)S(1)} %copy-done.27, bf16[512,512]{1,0:T(8,128)(2,1)S(1)} %convolution_convert_fusion.1.grad_ref), custom_call_target="tpu_custom_call" | custom-call | flops 1 | bytes 1 | tf_op jit(solution)/shard_map/pallas_call | solution.py:349
  290.3 4.8 collective-permute-done.34
  307.2 4.1 collective-permute-done.36
  311.3 3.8 multiply_reduce_fusion.3
  342.9 14.3 %collective-permute-done.38 = f32[512,512]{1,0:T(8,128)} collective-permute-done((f32[512,512]{1,0:T(8,128)}, f32[512,512]{1,0:T(8,128)}, u32[]{:S(2)}, u32[]{:S(2)}) %collective-permute-start.38) | collective-permute-done | bytes 1048608 | tf_op jit(solution)/shard_map/ppermute | solution.py:50
  378.8 18.7 %collective-permute-done.42 = f32[256,1024]{1,0:T(8,128)} collective-permute-done((f32[256,1024]{1,0:T(8,128)}, f32[256,1024]{1,0:T(8,128)}, u32[]{:S(2)}, u32[]{:S(2)}) %collective-permute-start.42) | collective-permute-done | bytes 1048608 | tf_op jit(solution)/shard_map/ppermute | solution.py:50
  410.2 5.8 %collective-permute-done.46 = f32[64,2048]{1,0:T(8,128)S(1)} collective-permute-done((f32[64,2048]{1,0:T(8,128)S(1)}, f32[64,2048]{1,0:T(8,128)S(1)}, u32[]{:S(2)}, u32[]{:S(2)}) %collective-permute-start.46) | collective-permute-done | bytes 524320 | tf_op jit(solution)/shard_map/ppermute | solution.py:50
  416.0 8.6 %collective-permute-done.45 = f32[64,2048]{1,0:T(8,128)S(1)} collective-permute-done((f32[64,2048]{1,0:T(8,128)S(1)}, f32[64,2048]{1,0:T(8,128)S(1)}, u32[]{:S(2)}, u32[]{:S(2)}) %collective-permute-start.45) | collective-permute-done | bytes 524320 | tf_op jit(solution)/shard_map/ppermute | solution.py:50
  438.9 10.6 %collective-permute-start.56 = (f32[128,512]{1,0:T(8,128)S(1)}, f32[128,512]{1,0:T(8,128)S(1)}, u32[]{:S(2)}, u32[]{:S(2)}) collective-permute-start(f32[128,512]{1,0:T(8,128)S(1)} %dynamic-slice_bitcast_fusion.9), channel_id=1, source_target_pairs={{0,8},{1,9},{2,26},{3,27},{4,12},{5,13},{6,30},{7,31},{8,16},{9,17... | collective-permute-start | bytes 786440 | tf_op jit(solution)/shard_map/ppermute | solution.py:50
  456.7 5.7 collective-permute-done.55
  476.3 4.4 collective-permute-done.66
  522.9 15.2 %collective-permute-start.79 = (f32[3,128]{1,0:T(4,128)S(1)}, f32[3,128]{1,0:T(4,128)S(1)}, u32[]{:S(2)}, u32[]{:S(2)}) collective-permute-start(f32[3,128]{1,0:T(4,128)S(1)} %broadcast_in_dim.95), channel_id=1, source_target_pairs={{0,2},{1,3},{2,0},{3,1},{4,6},{5,7},{6,4},{7,5},{8,10},{9,11},{10,... | collective-permute-start | bytes 4616 | tf_op jit(solution)/shard_map/ppermute | solution.py:50
  552.0 4.0 collective-permute-start.89
  (663 shorter events, 367.6 us)
Async XLA Ops:
  7.2 390.3 %reduce-scatter.3.cloned.1.call-start = ((), (), s32[]{:S(2)}) async-start(), calls=%async_computation.2 | async-start | bytes 10485760 | tf_op jit(solution)/shard_map/reduce_scatter | solution.py:218
  13.0 19.5 %collective-permute-start.1 = (f32[64,2816]{1,0:T(8,128)}, f32[64,2816]{1,0:T(8,128)S(1)}, u32[]{:S(2)}, u32[]{:S(2)}) collective-permute-start(f32[64,2816]{1,0:T(8,128)} %fusion.62), channel_id=1, source_target_pairs={{0,5},{1,4},{2,7},{3,6},{4,1},{5,0},{6,3},{7,2},{8,13},{9,12},{10,... | collective-permute-start | bytes 2162696 | tf_op jit(solution)/shard_map/ppermute | solution.py:50
  36.3 28.4 %collective-permute-start.8 = (f32[512,1024]{1,0:T(8,128)S(1)}, f32[512,1024]{1,0:T(8,128)S(1)}, u32[]{:S(2)}, u32[]{:S(2)}) collective-permute-start(f32[512,1024]{1,0:T(8,128)S(1)} %pad_maximum_fusion), channel_id=1, source_target_pairs={{1,0},{2,3},{5,4},{6,7},{9,8},{10,11},{13,12},{14,15},{17,16},{18,... | collective-permute-start | bytes 6291464 | tf_op jit(solution)/shard_map/ppermute | solution.py:50
  99.0 23.9 %collective-permute-start.18 = (f32[512,512]{1,0:T(8,128)}, f32[512,512]{1,0:T(8,128)}, u32[]{:S(2)}, u32[]{:S(2)}) collective-permute-start(f32[512,512]{1,0:T(8,128)} %bitcast_convert_fusion), channel_id=1, source_target_pairs={{0,5},{1,4},{2,7},{3,6},{4,1},{5,0},{6,3},{7,2},{8,13},{9,12},{10,... | collective-permute-start | bytes 3145736 | tf_op jit(solution)/shard_map/ppermute | solution.py:50
  126.1 22.1 %collective-permute-start.21 = (f32[512,512]{1,0:T(8,128)}, f32[512,512]{1,0:T(8,128)}, u32[]{:S(2)}, u32[]{:S(2)}) collective-permute-start(f32[512,512]{1,0:T(8,128)} %collective-permute-done.18.near_ref), channel_id=1, source_target_pairs={{0,4},{1,5},{2,6},{3,7},{4,0},{5,1},{6,2},{7,3},{8,12},{9,13},{10,... | collective-permute-start | bytes 3145736 | tf_op jit(solution)/shard_map/ppermute | solution.py:50
  164.8 17.4 %collective-permute-start.24 = (f32[512,1024]{1,0:T(8,128)}, f32[512,1024]{1,0:T(8,128)}, u32[]{:S(2)}, u32[]{:S(2)}) collective-permute-start(f32[512,1024]{1,0:T(8,128)} %fusion.135), channel_id=1, source_target_pairs={{0,2},{1,3},{2,0},{3,1},{4,6},{5,7},{6,4},{7,5},{8,10},{9,11},{10,... | collective-permute-start | bytes 6291464 | tf_op jit(solution)/shard_map/ppermute | solution.py:50
  174.8 21.0 %collective-permute-start.28 = (f32[512,256]{1,0:T(8,128)S(1)}, f32[512,256]{1,0:T(8,128)S(1)}, u32[]{:S(2)}, u32[]{:S(2)}) collective-permute-start(f32[512,256]{1,0:T(8,128)S(1)} %convert_select_fusion.3), channel_id=1, source_target_pairs={{0,1},{1,0},{2,3},{3,2},{4,5},{5,4},{6,7},{7,6},{8,9},{9,8},{10,11... | collective-permute-start | bytes 1572872 | tf_op jit(solution)/shard_map/ppermute | solution.py:50
  237.5 198.4 %reduce-scatter.5.cloned.1.call-start = ((), (), s32[]{:S(2)}) async-start(), calls=%async_computation.3 | async-start | bytes 5242880 | tf_op jit(solution)/shard_map/reduce_scatter | solution.py:218
  237.5 20.7 %collective-permute-start.32 = (f32[512,512]{1,0:T(8,128)}, f32[512,512]{1,0:T(8,128)}, u32[]{:S(2)}, u32[]{:S(2)}) collective-permute-start(f32[512,512]{1,0:T(8,128)} %fusion.45), channel_id=1, source_target_pairs={{0,4},{1,5},{2,7},{3,6},{4,1},{5,0},{6,2},{7,3},{8,12},{9,13},{10,... | collective-permute-start | bytes 3145736 | tf_op jit(solution)/shard_map/ppermute | solution.py:50
  268.6 21.7 %collective-permute-start.35 = (f32[512,512]{1,0:T(8,128)S(1)}, f32[512,512]{1,0:T(8,128)S(1)}, u32[]{:S(2)}, u32[]{:S(2)}) collective-permute-start(f32[512,512]{1,0:T(8,128)S(1)} %convolution_add_fusion), channel_id=1, source_target_pairs={{0,4},{1,5},{2,7},{3,6},{4,1},{5,0},{6,2},{7,3},{8,12},{9,13},{10,... | collective-permute-start | bytes 3145736 | tf_op jit(solution)/shard_map/ppermute | solution.py:50
  269.4 25.8 %collective-permute-start.34 = (f32[256,2048]{1,0:T(8,128)S(1)}, f32[256,2048]{1,0:T(8,128)S(1)}, u32[]{:S(2)}, u32[]{:S(2)}) collective-permute-start(f32[256,2048]{1,0:T(8,128)S(1)} %fusion.138), channel_id=1, source_target_pairs={{0,8},{1,9},{2,26},{3,27},{4,12},{5,13},{6,30},{7,31},{8,16},{9,17... | collective-permute-start | bytes 6291464 | tf_op jit(solution)/shard_map/ppermute | solution.py:50
  323.4 33.7 %collective-permute-start.37 = (f32[256,2048]{1,0:T(8,128)}, f32[256,2048]{1,0:T(8,128)}, u32[]{:S(2)}, u32[]{:S(2)}) collective-permute-start(f32[256,2048]{1,0:T(8,128)} %add.763), channel_id=1, source_target_pairs={{0,8},{1,9},{2,26},{3,27},{4,12},{5,13},{6,30},{7,31},{8,16},{9,17... | collective-permute-start | bytes 6291464 | tf_op jit(solution)/shard_map/ppermute | solution.py:50
  325.3 31.9 %collective-permute-start.39 = (f32[512,768]{1,0:T(8,128)}, f32[512,768]{1,0:T(8,128)}, u32[]{:S(2)}, u32[]{:S(2)}) collective-permute-start(f32[512,768]{1,0:T(8,128)} %fusion.31), channel_id=1, source_target_pairs={{0,4},{1,5},{2,7},{3,6},{4,1},{5,0},{6,2},{7,3},{8,12},{9,13},{10,... | collective-permute-start | bytes 4718600 | tf_op jit(solution)/shard_map/ppermute | solution.py:50
  330.6 26.6 %collective-permute-start.38 = (f32[512,512]{1,0:T(8,128)}, f32[512,512]{1,0:T(8,128)}, u32[]{:S(2)}, u32[]{:S(2)}) collective-permute-start(f32[512,512]{1,0:T(8,128)} %fusion.132), channel_id=1, source_target_pairs={{0,4},{1,5},{2,7},{3,6},{4,1},{5,0},{6,2},{7,3},{8,12},{9,13},{10,... | collective-permute-start | bytes 3145736 | tf_op jit(solution)/shard_map/ppermute | solution.py:50
  360.4 37.1 %collective-permute-start.40 = (f32[256,2048]{1,0:T(8,128)}, f32[256,2048]{1,0:T(8,128)}, u32[]{:S(2)}, u32[]{:S(2)}) collective-permute-start(f32[256,2048]{1,0:T(8,128)} %add.773), channel_id=1, source_target_pairs={{0,8},{1,9},{2,26},{3,27},{4,12},{5,13},{6,30},{7,31},{8,16},{9,17... | collective-permute-start | bytes 6291464 | tf_op jit(solution)/shard_map/ppermute | solution.py:50
  364.1 33.4 %collective-permute-start.41 = (f32[512,768]{1,0:T(8,128)}, f32[512,768]{1,0:T(8,128)}, u32[]{:S(2)}, u32[]{:S(2)}) collective-permute-start(f32[512,768]{1,0:T(8,128)} %add.774), channel_id=1, source_target_pairs={{0,4},{1,5},{2,7},{3,6},{4,1},{5,0},{6,2},{7,3},{8,12},{9,13},{10,... | collective-permute-start | bytes 4718600 | tf_op jit(solution)/shard_map/ppermute | solution.py:50
  370.3 27.2 %collective-permute-start.42 = (f32[256,1024]{1,0:T(8,128)}, f32[256,1024]{1,0:T(8,128)}, u32[]{:S(2)}, u32[]{:S(2)}) collective-permute-start(f32[256,1024]{1,0:T(8,128)} %pad_maximum_fusion.3), channel_id=1, source_target_pairs={{0,8},{1,9},{2,26},{3,27},{4,12},{5,13},{6,30},{7,31},{8,16},{9,17... | collective-permute-start | bytes 3145736 | tf_op jit(solution)/shard_map/ppermute | solution.py:50
  374.0 36.1 %collective-permute-start.47 = (f32[6,1024]{1,0:T(8,128)S(1)}, f32[6,1024]{1,0:T(8,128)S(1)}, u32[]{:S(2)}, u32[]{:S(2)}) collective-permute-start(f32[6,1024]{1,0:T(8,128)S(1)} %stack.126), channel_id=1, source_target_pairs={{0,8},{1,9},{2,10},{3,11},{4,12},{5,13},{6,14},{7,15},{8,0},{9,1},... | collective-permute-start | bytes 73736 | tf_op jit(solution)/shard_map/ppermute | solution.py:50
  399.6 25.0 %collective-permute-start.43 = (f32[512,768]{1,0:T(8,128)S(1)}, f32[512,768]{1,0:T(8,128)S(1)}, u32[]{:S(2)}, u32[]{:S(2)}) collective-permute-start(f32[512,768]{1,0:T(8,128)S(1)} %add.775), channel_id=1, source_target_pairs={{0,4},{1,5},{2,7},{3,6},{4,1},{5,0},{6,2},{7,3},{8,12},{9,13},{10,... | collective-permute-start | bytes 4718600 | tf_op jit(solution)/shard_map/ppermute | solution.py:50
  405.0 19.6 %collective-permute-start.44 = (f32[256,1024]{1,0:T(8,128)S(1)}, f32[256,1024]{1,0:T(8,128)S(1)}, u32[]{:S(2)}, u32[]{:S(2)}) collective-permute-start(f32[256,1024]{1,0:T(8,128)S(1)} %maximum_add_fusion), channel_id=1, source_target_pairs={{0,8},{1,9},{2,26},{3,27},{4,12},{5,13},{6,30},{7,31},{8,16},{9,17... | collective-permute-start | bytes 3145736 | tf_op jit(solution)/shard_map/ppermute | solution.py:50
  425.5 24.1 %collective-permute-start.50 = (f32[64,2048]{1,0:T(8,128)}, f32[64,2048]{1,0:T(8,128)S(1)}, u32[]{:S(2)}, u32[]{:S(2)}) collective-permute-start(f32[64,2048]{1,0:T(8,128)} %bitcast_add_fusion.4), channel_id=1, source_target_pairs={{0,32},{1,33},{2,98},{3,99},{4,36},{5,37},{6,102},{7,103},{8,40},{... | collective-permute-start | bytes 1572872 | tf_op jit(solution)/shard_map/ppermute | solution.py:50
  426.9 22.7 %collective-permute-start.48 = (f32[256,1024]{1,0:T(8,128)}, f32[256,1024]{1,0:T(8,128)}, u32[]{:S(2)}, u32[]{:S(2)}) collective-permute-start(f32[256,1024]{1,0:T(8,128)} %maximum_add_fusion.1), channel_id=1, source_target_pairs={{0,8},{1,9},{2,26},{3,27},{4,12},{5,13},{6,30},{7,31},{8,16},{9,17... | collective-permute-start | bytes 3145736 | tf_op jit(solution)/shard_map/ppermute | solution.py:50
  429.3 20.2 %collective-permute-start.49 = (f32[64,2048]{1,0:T(8,128)}, f32[64,2048]{1,0:T(8,128)}, u32[]{:S(2)}, u32[]{:S(2)}) collective-permute-start(f32[64,2048]{1,0:T(8,128)} %bitcast_add_fusion.5), channel_id=1, source_target_pairs={{0,8},{1,9},{2,26},{3,27},{4,12},{5,13},{6,30},{7,31},{8,16},{9,17... | collective-permute-start | bytes 1572872 | tf_op jit(solution)/shard_map/ppermute | solution.py:50
  430.4 19.2 %collective-permute-start.51 = (f32[128,768]{1,0:T(8,128)}, f32[128,768]{1,0:T(8,128)S(1)}, u32[]{:S(2)}, u32[]{:S(2)}) collective-permute-start(f32[128,768]{1,0:T(8,128)} %dynamic-slice_bitcast_fusion.5), channel_id=1, source_target_pairs={{0,32},{1,33},{2,98},{3,99},{4,36},{5,37},{6,102},{7,103},{8,40},{... | collective-permute-start | bytes 1179656 | tf_op jit(solution)/shard_map/ppermute | solution.py:50
  (199 other events, 1695.1 us)
Sparse Core Ops, SparseCore 0:
  237.6 78.6 reduce-scatter.2
  323.5 44.0 reduce-scatter.4
